TPU v7x, 128 devices: a whole 4x4x4 slice. The times are simulated.
128 devices in a mesh: gx: 8 (over x, y_lo), gy: 16 (over y_hi, z, core).
Axes of the slice: x: 4, y: 4 (y_hi: 2, y_lo: 2; y = y_hi * 2 + y_lo), z: 4, core: 2. Of those that a mesh axis runs over, the one named last changes fastest.
Arguments:
- biomass: float32 [256, 256, 2048], P(None, 'gx', 'gy'), may hold values from 0.05 to 2
- capacity: float32 [256, 2048], P('gx', 'gy'), may hold values from 0.5 to 4
- adjacency: int32 [256, 256], replicated, may hold values 0 or 1
- trophic_level: int32 [256], replicated, may hold values from 0 to 3
- attack: float32 [256], replicated, may hold values from 0.05 to 0.5
- disp_rate: float32 [256], replicated, may hold values from 0.5 to 6
- disp_len: float32 [256], replicated, may hold values from 50 to 400
Outputs:
- advanced: float32 [256, 256, 2048], P(None, 'gx', 'gy')
Inputs may be any that keep to these rules, and one draw needn't show every extreme that they name: `adjacency`: 0/1 feeding links.
All inputs are finite; a program needn't handle non-finite values.
Results may differ from a plain program's by a relative error of at most 0.000071.
Values sent between devices are 32-bit elements; how exact they have to be, the bound alone decides.
No kernel may reach another device: no remote copies, remote signals or barrier semaphores. Data moves between devices by JAX's collectives and lax.ppermute only.
A program may use at most 128 MiB of HBM per device.

v0:
```python
import jax
import jax.numpy as jnp
from jax import lax
from jax.sharding import PartitionSpec as P

time_step = 0.25
handling = 1.0
efficiency = 0.6
mortal_rate = 0.15


def shifted(value, axis, steps):
    count = lax.axis_size(axis)
    first, last = (max(0, -steps), min(count, count - steps))
    return lax.ppermute(value, axis, [(source, source + steps) for source in range(first, last)])


def local_kernels(inverse, count):
    places = jnp.arange(count, dtype=jnp.float32)
    spacing = jnp.abs(places[:, None] - places[None, :])
    square = jnp.exp(-spacing[None] * inverse[:, None, None])
    leading = jnp.exp(-(places[None] + 1.0) * inverse[:, None])
    trailing = jnp.exp(-(count - places[None]) * inverse[:, None])
    tail_front = jnp.exp(-(count - 1.0 - places[None]) * inverse[:, None])
    tail_back = jnp.exp(-places[None] * inverse[:, None])
    across = jnp.exp(-count * inverse)[:, None]
    return (square, leading, trailing, tail_front, tail_back, across)


def sweep_columns(values, inverse, scale):
    count = values.shape[1]
    square, leading, trailing, tail_front, tail_back, across = local_kernels(inverse, count)
    inner = jnp.einsum("sij,sjy->siy", square, values, precision=lax.Precision.HIGHEST)
    front = jnp.einsum("sj,sjy->sy", tail_front, values, precision=lax.Precision.HIGHEST)
    back = jnp.einsum("sj,sjy->sy", tail_back, values, precision=lax.Precision.HIGHEST)
    links = lax.axis_size("gx")

    def east_step(turn, carry):
        return shifted(across * carry + front, "gx", 1)

    def west_step(turn, carry):
        return shifted(across * carry + back, "gx", -1)

    carry_front = lax.fori_loop(0, links - 1, east_step, jnp.zeros_like(front))
    carry_back = lax.fori_loop(0, links - 1, west_step, jnp.zeros_like(back))
    total = (
        inner
        + leading[:, :, None] * carry_front[:, None, :]
        + trailing[:, :, None] * carry_back[:, None, :]
    )
    return scale[:, None, None] * total


def sweep_rows(values, inverse, scale):
    count = values.shape[2]
    square, leading, trailing, tail_front, tail_back, across = local_kernels(inverse, count)
    inner = jnp.einsum("sij,sxj->sxi", square, values, precision=lax.Precision.HIGHEST)
    front = jnp.einsum("sj,sxj->sx", tail_front, values, precision=lax.Precision.HIGHEST)
    back = jnp.einsum("sj,sxj->sx", tail_back, values, precision=lax.Precision.HIGHEST)
    links = lax.axis_size("gy")

    def north_step(turn, carry):
        return shifted(across * carry + front, "gy", 1)

    def south_step(turn, carry):
        return shifted(across * carry + back, "gy", -1)

    carry_front = lax.fori_loop(0, links - 1, north_step, jnp.zeros_like(front))
    carry_back = lax.fori_loop(0, links - 1, south_step, jnp.zeros_like(back))
    total = (
        inner
        + leading[:, None, :] * carry_front[:, :, None]
        + trailing[:, None, :] * carry_back[:, :, None]
    )
    return scale[:, None, None] * total


def respond(values, capacity, weights, basal, level_float):
    species = values.shape[0]
    flattened = values.reshape(species, -1)
    positive = jnp.maximum(flattened, 0.0)
    grazing = jnp.dot(
        weights.T, positive, precision=lax.Precision.HIGHEST, preferred_element_type=jnp.float32
    )
    handled = positive / (1.0 + handling * grazing)
    losses = positive * jnp.dot(
        weights, handled, precision=lax.Precision.HIGHEST, preferred_element_type=jnp.float32
    )
    growth = basal[:, None] * positive * (1.0 - positive / capacity.reshape(1, -1))
    result = (
        growth
        + efficiency * handled * grazing
        - losses
        - mortal_rate * level_float[:, None] * positive
    )
    return result.reshape(values.shape)


def shards(biomass, capacity, adjacency, trophic_level, attack, disp_rate, disp_len):
    inverse = 1.0 / disp_len
    decay = jnp.exp(-inverse)
    scale = (1.0 - decay) / (1.0 + decay)
    weights = adjacency.astype(jnp.float32) * attack[None, :]
    basal = (trophic_level == 0).astype(jnp.float32)
    level_float = trophic_level.astype(jnp.float32)

    def evaluate(state):
        smooth = sweep_rows(sweep_columns(state, inverse, scale), inverse, scale)
        return respond(state, capacity, weights, basal, level_float) + disp_rate[:, None, None] * (
            smooth - state
        )

    first = evaluate(biomass)
    middle = biomass + time_step * first
    second = evaluate(middle)
    return biomass + 0.5 * time_step * (first + second)


def solution(mesh):
    return jax.shard_map(
        shards,
        mesh=mesh,
        in_specs=(P(None, "gx", "gy"), P("gx", "gy"), P(), P(), P(), P(), P()),
        out_specs=P(None, "gx", "gy"),
        check_vma=False,
    )
```

profile of v0, /device:TPU:22, one launch (start us, length us, event | category | flops | bytes accessed | tf_op | source)
XLA Modules:
  0.0 997.2 jit_solution(13902192430128094061)
XLA Ops:
  6.3 54.9 %while.81 = (s32[]{:T(128)}, f32[256,128]{1,0:T(8,128)S(1)}, f32[256,1]{0,1:T(1,128)S(1)}, f32[256,128]{1,0:T(8,128)S(1)}, s32[]{:T(128)}) while((s32[]{:T(128)}, f32[256,128]{1,0:T(8,128)S(1)}, f32[256,1]{0,1:T(1,128)S(1)}, f32[256,128]{1,0:T(8,128)S(1)}, s32[]{:T(128)}) %tuple.159), condition=%wide.region_3.0_spmd, body=%wide.region_2.0_spmd.sunk | while | flops 65538 | bytes 918629 | solution.py:45
  66.6 56.6 %while.80 = (s32[]{:T(128)}, f32[256,128]{1,0:T(8,128)S(1)}, f32[256,1]{0,1:T(1,128)S(1)}, f32[256,128]{1,0:T(8,128)S(1)}, s32[]{:T(128)}) while((s32[]{:T(128)}, f32[256,128]{1,0:T(8,128)S(1)}, f32[256,1]{0,1:T(1,128)S(1)}, f32[256,128]{1,0:T(8,128)S(1)}, s32[]{:T(128)}) %tuple.160), condition=%wide.region_1.0_spmd, body=%wide.region_0.0_spmd.sunk | while | flops 65538 | bytes 918629 | solution.py:44
  123.3 8.7 add_multiply_fusion.1
  140.7 144.6 %while.83 = (s32[]{:T(128)}, f32[256,32]{1,0:T(8,128)S(1)}, f32[256,1]{0,1:T(1,128)S(1)}, f32[256,32]{1,0:T(8,128)S(1)}, s32[]{:T(128)}) while((s32[]{:T(128)}, f32[256,32]{1,0:T(8,128)S(1)}, f32[256,1]{0,1:T(1,128)S(1)}, f32[256,32]{1,0:T(8,128)S(1)}, s32[]{:T(128)}) %tuple.155), condition=%wide.region_7.0_spmd, body=%wide.region_6.0_spmd.sunk | while | flops 16386 | bytes 230501 | solution.py:69
  175.4 7.4 collective-permute-start.3
  215.4 7.4 collective-permute-start.3
  285.3 8.6 fusion.47
  293.9 150.2 %while.82 = (s32[]{:T(128)}, f32[256,32]{1,0:T(8,128)S(1)}, f32[256,1]{0,1:T(1,128)S(1)}, f32[256,32]{1,0:T(8,128)S(1)}, s32[]{:T(128)}) while((s32[]{:T(128)}, f32[256,32]{1,0:T(8,128)S(1)}, f32[256,1]{0,1:T(1,128)S(1)}, f32[256,32]{1,0:T(8,128)S(1)}, s32[]{:T(128)}) %tuple.156), condition=%wide.region_5.0_spmd, body=%wide.region_4.0_spmd.sunk | while | flops 16386 | bytes 230501 | solution.py:68
  295.9 8.1 collective-permute-done.2
  306.1 8.0 collective-permute-done.2
  316.1 8.0 collective-permute-done.2
  326.1 8.0 collective-permute-done.2
  336.1 8.0 collective-permute-done.2
  346.1 8.0 collective-permute-done.2
  356.1 8.0 collective-permute-done.2
  366.1 8.0 collective-permute-done.2
  376.1 8.0 collective-permute-done.2
  386.1 8.0 collective-permute-done.2
  396.1 8.0 collective-permute-done.2
  406.1 8.0 collective-permute-done.2
  416.1 8.0 collective-permute-done.2
  426.1 8.0 collective-permute-done.2
  436.1 8.0 collective-permute-done.2
  453.1 20.6 %fusion.32 = f32[32,8,32,128]{3,1,2,0:T(8,128)S(1)} fusion(f32[256,4096]{1,0:T(8,128)S(1)} %fusion.18, f32[32,8,32,128]{3,2,1,0:T(8,128)S(1)} %bitcast.169, f32[256]{0:T(256)S(1)} %convert_multiply_fusion.5, f32[4096]{0:T(1024)S(1)} %bitcast.192, f32[256]{0:T(256)S(1)} %compare_convert_fusion, s32[256,256]{1,0:T(8,128)S(1)} %copy-done.5, f32[256]{0:T(256)S(1)} %copy-done.7), kind=kOutput, calls=%fused_computation.57 | convolution fusion | flops 3237085184 | bytes 12864512 | tf_op jit(solution)/shard_map/dot_general | solution.py:86
  478.8 29.2 %broadcast_maximum_fusion = (f32[256,32,128]{2,1,0:T(8,128)S(1)}, f32[256,32,128]{2,1,0:T(8,128)}, f32[256,32,128]{2,1,0:T(8,128)}) fusion(f32[256,32,128]{2,1,0:T(8,128)S(1)} %copy-done, f32[256,32]{1,0:T(8,128)S(1)} %get-tuple-element.184, f32[256,128]{1,0:T(8,128)S(1)} %get-tuple-element.259, f32[256,32]{1,0:T(8,128)S(1)} %get-tuple-element.183, ...), kind=kOutput, calls=%fused_computation.64 | convolution fusion | flops 1626341376 | bytes 25562112 | tf_op jit(solution)/shard_map/sij,sxj->sxi/dot_general | solution.py:57
  514.2 9.9 fusion.31
  532.0 52.6 %while.85 = (s32[]{:T(128)}, f32[256,128]{1,0:T(8,128)S(1)}, f32[256,1]{0,1:T(1,128)S(1)}, f32[256,128]{1,0:T(8,128)S(1)}, s32[]{:T(128)}) while((s32[]{:T(128)}, f32[256,128]{1,0:T(8,128)S(1)}, f32[256,1]{0,1:T(1,128)S(1)}, f32[256,128]{1,0:T(8,128)S(1)}, s32[]{:T(128)}) %tuple.161), condition=%wide.region_11.0_spmd, body=%wide.region_10.0_spmd.sunk | while | flops 65538 | bytes 918629 | solution.py:45
  589.8 55.5 %while.84 = (s32[]{:T(128)}, f32[256,128]{1,0:T(8,128)S(1)}, f32[256,1]{0,1:T(1,128)S(1)}, f32[256,128]{1,0:T(8,128)S(1)}, s32[]{:T(128)}) while((s32[]{:T(128)}, f32[256,128]{1,0:T(8,128)S(1)}, f32[256,1]{0,1:T(1,128)S(1)}, f32[256,128]{1,0:T(8,128)S(1)}, s32[]{:T(128)}) %tuple.162), condition=%wide.region_9.0_spmd, body=%wide.region_8.0_spmd.sunk | while | flops 65538 | bytes 918629 | solution.py:44
  645.4 8.9 add_multiply_fusion
  662.9 144.6 %while.87 = (s32[]{:T(128)}, f32[256,32]{1,0:T(8,128)S(1)}, f32[256,1]{0,1:T(1,128)S(1)}, f32[256,32]{1,0:T(8,128)S(1)}, s32[]{:T(128)}) while((s32[]{:T(128)}, f32[256,32]{1,0:T(8,128)S(1)}, f32[256,1]{0,1:T(1,128)S(1)}, f32[256,32]{1,0:T(8,128)S(1)}, s32[]{:T(128)}) %tuple.157), condition=%wide.region_15.0_spmd, body=%wide.region_14.0_spmd.sunk | while | flops 16386 | bytes 230501 | solution.py:69
  807.5 8.3 fusion.51
  815.8 150.2 %while.86 = (s32[]{:T(128)}, f32[256,32]{1,0:T(8,128)S(1)}, f32[256,1]{0,1:T(1,128)S(1)}, f32[256,32]{1,0:T(8,128)S(1)}, s32[]{:T(128)}) while((s32[]{:T(128)}, f32[256,32]{1,0:T(8,128)S(1)}, f32[256,1]{0,1:T(1,128)S(1)}, f32[256,32]{1,0:T(8,128)S(1)}, s32[]{:T(128)}) %tuple.158), condition=%wide.region_13.0_spmd, body=%wide.region_12.0_spmd.sunk | while | flops 16386 | bytes 230501 | solution.py:68
  817.9 8.1 collective-permute-done.6
  828.0 8.0 collective-permute-done.6
  838.0 8.0 collective-permute-done.6
  848.0 8.0 collective-permute-done.6
  858.0 8.0 collective-permute-done.6
  868.0 8.0 collective-permute-done.6
  878.0 8.0 collective-permute-done.6
  888.0 8.0 collective-permute-done.6
  898.0 8.0 collective-permute-done.6
  908.0 8.0 collective-permute-done.6
  918.0 8.0 collective-permute-done.6
  928.0 8.0 collective-permute-done.6
  938.0 8.0 collective-permute-done.6
  948.1 8.0 collective-permute-done.6
  958.1 8.0 collective-permute-done.6
  966.0 30.9 %fusion.12 = f32[256,32,128]{2,1,0:T(8,128)} fusion(f32[256,32,128]{2,1,0:T(8,128)} %param.23, f32[32,8,32,128]{3,2,1,0:T(8,128)} %copy.25, f32[256,32,128]{2,1,0:T(8,128)} %get-tuple-element.254, f32[256,32,128]{2,1,0:T(8,128)} %get-tuple-element.267, f32[32,8,32,128]{3,2,1,0:T(8,128)} %copy-done.1, f32[256,32]{1,0:T(8,128)S(1)} %get-tuple-element.188, ...), kind=kOutput, calls=%fused_computation.24 | convolution fusion | flops 1634729984 | bytes 29821952 | tf_op jit(solution)/shard_map/sij,sxj->sxi/dot_general | solution.py:57
  (287 shorter events, 615.8 us)
Async XLA Ops:
  145.3 9.9 collective-permute-start.3
  155.4 9.9 collective-permute-start.3
  165.4 9.9 collective-permute-start.3
  175.4 9.9 collective-permute-start.3
  185.4 9.9 collective-permute-start.3
  195.4 9.9 collective-permute-start.3
  205.4 9.9 collective-permute-start.3
  215.4 9.9 collective-permute-start.3
  225.4 9.9 collective-permute-start.3
  235.4 9.9 collective-permute-start.3
  245.4 9.9 collective-permute-start.3
  255.4 9.9 collective-permute-start.3
  265.4 9.9 collective-permute-start.3
  275.4 9.9 collective-permute-start.3
  294.0 10.0 %collective-permute-start.2 = (f32[256,32]{1,0:T(8,128)S(1)}, f32[256,32]{1,0:T(8,128)S(1)}, u32[]{:S(2)}, u32[]{:S(2)}) collective-permute-start(f32[256,32]{1,0:T(8,128)S(1)} %multiply_add_fusion.20), channel_id=1, source_target_pairs={{0,1},{1,2},{2,3},{3,4},{4,5},{5,6},{6,7},{7,8},{8,9},{9,10},{10,1... | collective-permute-start | bytes 98312 | tf_op jit(solution)/shard_map/while/body/eval_jaxpr/ppermute | solution.py:15
  304.1 9.9 collective-permute-start.2
  314.1 9.9 collective-permute-start.2
  324.1 9.9 collective-permute-start.2
  334.1 9.9 collective-permute-start.2
  344.1 9.9 collective-permute-start.2
  354.2 9.9 collective-permute-start.2
  364.2 9.9 collective-permute-start.2
  374.2 9.9 collective-permute-start.2
  384.2 9.9 collective-permute-start.2
  394.2 9.9 collective-permute-start.2
  404.2 9.9 collective-permute-start.2
  414.2 9.9 collective-permute-start.2
  424.2 9.9 collective-permute-start.2
  434.2 9.9 collective-permute-start.2
  667.5 9.9 collective-permute-start.7
  677.5 9.9 collective-permute-start.7
  687.5 9.9 collective-permute-start.7
  697.5 9.9 collective-permute-start.7
  707.5 9.9 collective-permute-start.7
  717.5 9.9 collective-permute-start.7
  727.6 9.9 collective-permute-start.7
  737.6 9.9 collective-permute-start.7
  747.6 9.9 collective-permute-start.7
  757.6 9.9 collective-permute-start.7
  767.6 9.9 collective-permute-start.7
  777.6 9.9 collective-permute-start.7
  787.6 9.9 collective-permute-start.7
  797.6 9.9 collective-permute-start.7
  815.9 10.0 %collective-permute-start.6 = (f32[256,32]{1,0:T(8,128)S(1)}, f32[256,32]{1,0:T(8,128)S(1)}, u32[]{:S(2)}, u32[]{:S(2)}) collective-permute-start(f32[256,32]{1,0:T(8,128)S(1)} %multiply_add_fusion.24), channel_id=1, source_target_pairs={{0,1},{1,2},{2,3},{3,4},{4,5},{5,6},{6,7},{7,8},{8,9},{9,10},{10,1... | collective-permute-start | bytes 98312 | tf_op jit(solution)/shard_map/while/body/eval_jaxpr/ppermute | solution.py:15
  846.1 9.9 collective-permute-start.6
  896.1 9.9 collective-permute-start.6
  936.1 9.9 collective-permute-start.6
  946.1 9.9 collective-permute-start.6
  (50 other events, 393.2 us)
where the time goes:
time: 1000 us; the launch traced here: 997 us
  waiting for transfers between devices  439 us (44%)
  starting transfers between devices  361 us (36%)
  matrix products  171 us (17%)
  other arithmetic  12.4 us (1%)
  local copies, waits for them, and re-layouts  12.1 us (1%)
    ppermute x88, waiting for transfers between devices, shifted(): lax.ppermute(value, axis, [(source, source + steps) for source in range(f...  439 us
    ppermute x88, starting transfers between devices, shifted(): lax.ppermute(value, axis, [(source, source + steps) for source in range(f...  361 us
    dot_general x2, matrix products, sweep_rows(): jnp.einsum('sij,sxj->sxi', square, values, precision=lax.Precision.HIGHEST)  60.2 us
    dot_general x2, matrix products, respond(): jnp.dot(weights, handled, precision=lax.Precision.HIGHEST, preferred_elem...  30.5 us
  transfers between devices with their start and end apart: 88, of which 88 were waited for; matrix products, arithmetic and copies ran while one was open for 0% of the time, Pallas kernels for 0%

commit v1 on v0

v1 whole, which is shorter than its diff:
```python
import functools

import jax
import jax.numpy as jnp
from jax import lax
from jax.experimental import pallas as pl
from jax.experimental.pallas import tpu as pltpu
from jax.sharding import PartitionSpec as P

time_step = 0.25
handling = 1.0
efficiency = 0.6
mortal_rate = 0.15

S = 256
NXL = 32
NYL = 128
CH = 64
BX = 8
F32 = jnp.float32
BF16 = jnp.bfloat16
VMEM_LIMIT = 56 * 1024 * 1024


LAM, DEC, NORM2, RATE, ATT, BASAL, LEVEL = range(7)


def col(cols, k):
    return cols[:, k : k + 1]


def lanes(rows):
    return lax.broadcasted_iota(jnp.int32, (rows, NYL), 1)


def wide(column):
    return jnp.broadcast_to(column, (column.shape[0], NYL))


def powers(lam, exponent):
    return jnp.exp(-lam * exponent)


def tables(lam):
    y = lanes(lam.shape[0]).astype(F32) - 64.0
    return jnp.exp(-lam * y), jnp.exp(lam * y)


def second_tables(lam, dec):
    y = lanes(lam.shape[0]).astype(F32)
    inv = 1.0 / ((1.0 - dec) * (1.0 + dec))
    alpha = (y + 1.0) * jnp.exp(-lam * (y + 1.0)) + (jnp.exp(-lam * (y + 3.0)) - jnp.exp(-lam * (257.0 - y))) * inv
    beta = (128.0 - y) * jnp.exp(-lam * (128.0 - y)) + (jnp.exp(-lam * (130.0 - y)) - jnp.exp(-lam * (130.0 + y))) * inv
    return alpha, beta


def split(v):
    hi = v.astype(BF16)
    lo = (v - hi.astype(F32)).astype(BF16)
    return jnp.concatenate([hi, lo], axis=1)


def triangles():
    i = lax.broadcasted_iota(jnp.int32, (2 * NYL, NYL), 0) % NYL
    j = lax.broadcasted_iota(jnp.int32, (2 * NYL, NYL), 1)
    return (i <= j).astype(F32).astype(BF16), (i > j).astype(F32).astype(BF16)


def smooth_rows(v, a, ia, low, upp):
    f = jnp.dot(split(v * ia), low, preferred_element_type=F32)
    g = jnp.dot(split(v * a), upp, preferred_element_type=F32)
    return f * a + g * ia


def respond(v, rcap, adj, adj_t, att, basal, level):
    p = jnp.maximum(v, 0.0)
    both = jnp.dot(adj_t, split(p), preferred_element_type=F32)
    grazing = att * (both[:, :NYL] + both[:, NYL:])
    den = 1.0 + handling * grazing
    handled = p / den
    back = jnp.dot(adj, split(att * handled), preferred_element_type=F32)
    loss = back[:, :NYL] + back[:, NYL:]
    return p * (basal - mortal_rate * level - basal * p * rcap - loss) + efficiency * handled * grazing


def write_messages(msg_ref, front, back, lam, me, count, width):
    for k in range(count):
        gap = k - me
        dist = (jnp.abs(gap) - 1).astype(F32) * width
        w = jnp.exp(-lam * dist)
        picked = jnp.where(gap > 0, front, back)
        msg_ref[k] = jnp.where(gap == 0, 0.0, picked * w)


def read_carries(rx_ref, me, count):
    cf = jnp.zeros(rx_ref.shape[1:], F32)
    cb = jnp.zeros(rx_ref.shape[1:], F32)
    for k in range(count):
        m = rx_ref[k]
        cf = cf + jnp.where(k < me, m, 0.0)
        cb = cb + jnp.where(k > me, m, 0.0)
    return cf, cb


def fetch(b_hbm, bt, sems):
    for x in range(NXL):
        pltpu.make_async_copy(b_hbm.at[:, x, :], bt.at[x], sems.at[x]).start()


def fetched(b_hbm, bt, sems, x):
    pltpu.make_async_copy(b_hbm.at[:, x, :], bt.at[x], sems.at[x]).wait()


def tails_kernel(b_hbm, cols_ref, msg_ref, bt, fr, ba, sems):
    fetch(b_hbm, bt, sems)
    me = lax.axis_index("gx")
    for x0 in range(0, NXL, BX):
        for x in range(x0, x0 + BX):
            fetched(b_hbm, bt, sems, x)
        for s0 in range(0, S, CH):
            rows = pl.ds(s0, CH)
            lam = cols_ref[rows, LAM : LAM + 1]
            d = wide(cols_ref[rows, DEC : DEC + 1])
            vs = [bt[x, rows, :] for x in range(x0, x0 + BX)]
            f = fr[rows, :] if x0 else jnp.zeros((CH, NYL), F32)
            for v in vs:
                f = v + d * f
            g = vs[-1]
            for v in vs[-2::-1]:
                g = v + d * g
            fr[rows, :] = f
            if x0:
                ba[rows, :] = ba[rows, :] + powers(lam, float(x0)) * g
            else:
                ba[rows, :] = g
    write_messages(msg_ref, fr[...], ba[...], col(cols_ref[...], LAM), me, 8, float(NXL))


def first_kernel(b_hbm, adj_ref, cap_ref, cols_ref, q_ref, u_ref, fun_ref, bt, sems):
    fetch(b_hbm, bt, sems)
    cols = cols_ref[...]
    adj32 = adj_ref[...].astype(F32)
    adj = adj32.astype(BF16)
    adj_t = adj32.T.astype(BF16)
    att, basal, level, rate = (wide(col(cols, k)) for k in (ATT, BASAL, LEVEL, RATE))
    for x in range(NXL):
        fetched(b_hbm, bt, sems, x)

    def response(x, _):
        v = bt[x]
        rcap = 1.0 / cap_ref[pl.ds(x, 1), :]
        r = respond(v, rcap, adj, adj_t, att, basal, level)
        q_ref[x] = v + time_step * (r - rate * v)
        return 0

    lax.fori_loop(0, NXL, response, 0)

    def chunk(i, _):
        s0 = pl.multiple_of(i * CH, CH)
        rows = pl.ds(s0, CH)
        d = wide(cols_ref[rows, DEC : DEC + 1])
        lam = cols_ref[rows, LAM : LAM + 1]
        c = time_step * cols_ref[rows, RATE : RATE + 1] * cols_ref[rows, NORM2 : NORM2 + 1]
        y = lanes(CH).astype(F32)
        wf = jnp.exp(-lam * (127.0 - y))
        wb = jnp.exp(-lam * y)
        alpha, beta = second_tables(lam, cols_ref[rows, DEC : DEC + 1])
        inv_d = jnp.exp(lam)
        hf = c * beta * inv_d
        hb = c * alpha * inv_d
        lane = lanes(CH)

        def fwd(k, f):
            for j in range(BX):
                x = k * BX + j
                f = bt[x, rows, :] + d * f
                u_ref[x, rows, :] = f
            return f

        lax.fori_loop(0, NXL // BX, fwd, jnp.zeros((CH, NYL), F32))

        def bwd(k, carry):
            g, acc = carry
            for j in range(BX):
                x = NXL - 1 - (k * BX + j)
                g = d * g
                u = u_ref[x, rows, :] + g
                u_ref[x, rows, :] = u
                g = g + bt[x, rows, :]
                q = q_ref[x, rows, :]
                f1 = jnp.sum(wf * u, axis=1, keepdims=True)
                b1 = jnp.sum(wb * u, axis=1, keepdims=True)
                f2 = jnp.sum(wf * q + hf * u, axis=1, keepdims=True)
                b2 = jnp.sum(wb * q + hb * u, axis=1, keepdims=True)
                acc = jnp.where(lane == x, f1, acc)
                acc = jnp.where(lane == x + 32, f2, acc)
                acc = jnp.where(lane == x + 64, b1, acc)
                acc = jnp.where(lane == x + 96, b2, acc)
            return g, acc

        zero = jnp.zeros((CH, NYL), F32)
        _, acc = lax.fori_loop(0, NXL // BX, bwd, (zero, zero))
        fun_ref[rows, :] = acc
        return 0

    lax.fori_loop(0, S // CH, chunk, 0)


def by_group(lane, parts):
    out = parts[3]
    for k in (2, 1, 0):
        out = jnp.where(lane < 32 * (k + 1), parts[k], out)
    return out


def rows_kernel(rx_ref, fun_ref, cols_ref, car_ref, own_ref, msg_ref):
    mx, my = lax.axis_index("gx"), lax.axis_index("gy")
    cols = cols_ref[...]
    lam, dec = col(cols, LAM), col(cols, DEC)
    c = time_step * col(cols, RATE) * col(cols, NORM2)
    cf, cb = read_carries(rx_ref, mx, 8)
    car_ref[0] = cf
    car_ref[1] = cb
    lane = lanes(S)
    y = lane.astype(F32)
    wf = jnp.exp(-lam * (127.0 - y))
    wb = jnp.exp(-lam * y)
    alpha, beta = second_tables(lam, dec)
    inv_d = jnp.exp(lam)
    ws = (wf, c * beta * inv_d, wb, c * alpha * inv_d)
    pf = by_group(lane, [jnp.sum(w * cf, axis=1, keepdims=True) for w in ws])
    pb = by_group(lane, [jnp.sum(w * cb, axis=1, keepdims=True) for w in ws])
    xl = (lane % 32).astype(F32)
    fun = fun_ref[...] + jnp.exp(-lam * (xl + 1.0)) * pf + jnp.exp(-lam * (32.0 - xl)) * pb
    own_ref[...] = fun
    below, above = my.astype(F32), (15 - my).astype(F32)
    scale = c * dec / ((1.0 - dec) * (1.0 + dec)) * jnp.exp(-128.0 * lam)
    tb = scale * (1.0 - jnp.exp(-256.0 * below * lam))
    ta = scale * (1.0 - jnp.exp(-256.0 * above * lam))
    turned = pltpu.roll(fun, 96, 1)
    zero = jnp.zeros((S, 1), F32)
    fun = fun + by_group(lane, [zero, tb, zero, ta]) * turned
    shifted = by_group(lane, [zero, c * 128.0, zero, c * 128.0]) * pltpu.roll(fun, 32, 1)
    half = S // 2
    low_lanes = lanes(half) < 64

    def pack_front(v):
        return jnp.where(low_lanes, v[:half], pltpu.roll(v[half:], 64, 1))

    def pack_back(v):
        return jnp.where(low_lanes, pltpu.roll(v[:half], 64, 1), v[half:])

    f0, f1, b0, b1 = pack_front(fun), pack_front(shifted), pack_back(fun), pack_back(shifted)
    lam_p = jnp.where(low_lanes, lam[:half], lam[half:])
    for k in range(16):
        gap = k - my
        dist = (jnp.abs(gap) - 1).astype(F32)
        w = jnp.exp(-lam_p * (dist * 128.0))
        base = jnp.where(gap > 0, f0, b0) + dist * jnp.where(gap > 0, f1, b1)
        msg_ref[k] = jnp.where(gap == 0, 0.0, w * base)


def local_kernel(u_ref, q_ref, car_ref, cols_ref, mid_ref, p_ref, tail_ref, pf_ref, pb_ref):
    cols = cols_ref[...]
    lam = col(cols, LAM)
    c = wide(time_step * col(cols, RATE) * col(cols, NORM2))
    d = wide(col(cols, DEC))
    a, ia = tables(lam)
    low, upp = triangles()
    tail_ref[...] = jnp.zeros_like(tail_ref)
    pf_ref[...] = d
    pb_ref[...] = wide(jnp.exp(-32.0 * lam))
    inv_d = wide(jnp.exp(lam))

    def step(x, _):
        up, down = pf_ref[...], pb_ref[...]
        u = u_ref[x] + up * car_ref[0] + down * car_ref[1]
        mid = q_ref[x] + c * smooth_rows(u, a, ia, low, upp)
        mid_ref[x] = mid
        p = smooth_rows(mid, a, ia, low, upp)
        p_ref[x] = p
        tail_ref[0] = p + d * tail_ref[0]
        tail_ref[1] = tail_ref[1] + up * inv_d * p
        pf_ref[...] = up * d
        pb_ref[...] = down * inv_d
        return 0

    lax.fori_loop(0, NXL, step, 0)


def columns_kernel(ry_ref, own_ref, tail_ref, cols_ref, coef_ref, msg_ref):
    mx, my = lax.axis_index("gx"), lax.axis_index("gy")
    cols = cols_ref[...]
    lam, dec = col(cols, LAM), col(cols, DEC)
    c = time_step * col(cols, RATE) * col(cols, NORM2)
    lo, hi = read_carries(ry_ref, my, 16)
    half = S // 2
    low_lanes = lanes(half) < 64
    top = jnp.where(low_lanes, lo, pltpu.roll(hi, 64, 1))
    bottom = jnp.where(low_lanes, pltpu.roll(lo, 64, 1), hi)
    coef = jnp.concatenate([top, bottom], axis=0)
    lane = lanes(S)
    below, above = my.astype(F32), (15 - my).astype(F32)
    scale = c * dec / ((1.0 - dec) * (1.0 + dec))
    tb = scale * (1.0 - jnp.exp(-256.0 * below * lam))
    ta = scale * (1.0 - jnp.exp(-256.0 * above * lam))
    zero = jnp.zeros((S, 1), F32)
    turned = pltpu.roll(own_ref[...] + jnp.exp(-128.0 * lam) * coef, 96, 1)
    coef = coef + by_group(lane, [zero, tb, zero, ta]) * turned
    coef_ref[...] = coef
    xl = (lane % 32).astype(F32)
    cfx = coef * jnp.exp(-lam * (31.0 - xl))
    cbx = coef * jnp.exp(-lam * xl)
    y = lane.astype(F32)
    alpha, beta = second_tables(lam, dec)
    tabs = (c * alpha, jnp.exp(-lam * (y + 1.0)), c * beta, jnp.exp(-lam * (128.0 - y)))
    front, back = tail_ref[0], tail_ref[1]
    for k in range(4):
        inside = (lane >= 32 * k) & (lane < 32 * (k + 1))
        front = front + jnp.sum(jnp.where(inside, cfx, 0.0), axis=1, keepdims=True) * tabs[k]
        back = back + jnp.sum(jnp.where(inside, cbx, 0.0), axis=1, keepdims=True) * tabs[k]
    write_messages(msg_ref, front, back, lam, mx, 8, float(NXL))


def second_kernel(b_hbm, adj_ref, cap_ref, cols_ref, mid_ref, p_ref, coef_ref, out_ref, bt, v_ref, roll_ref, sems):
    fetch(b_hbm, bt, sems)
    cols = cols_ref[...]
    lam = col(cols, LAM)
    adj32 = adj_ref[...].astype(F32)
    adj = adj32.astype(BF16)
    adj_t = adj32.T.astype(BF16)
    att, basal, level, rate = (wide(col(cols, k)) for k in (ATT, BASAL, LEVEL, RATE))
    c = wide(time_step * col(cols, RATE) * col(cols, NORM2))
    y = lanes(S).astype(F32)
    ef = jnp.exp(-lam * (y + 1.0))
    eb = jnp.exp(-lam * (128.0 - y))
    alpha, beta = second_tables(lam, col(cols, DEC))
    roll_ref[...] = coef_ref[...]
    for x in range(NXL):
        fetched(b_hbm, bt, sems, x)

    def response(x, _):
        coef = roll_ref[...]
        cfu, cfm, cbu, cbm = (coef[:, 32 * k : 32 * k + 1] for k in range(4))
        roll_ref[...] = pltpu.roll(coef, 127, 1)
        mid = mid_ref[x] + c * (cfu * ef + cbu * eb)
        v_ref[x] = p_ref[x] + c * (cfu * alpha + cbu * beta) + cfm * ef + cbm * eb
        rcap = 1.0 / cap_ref[pl.ds(x, 1), :]
        r = respond(mid, rcap, adj, adj_t, att, basal, level)
        out_ref[x] = 0.5 * (bt[x] + mid) + 0.5 * time_step * (r - rate * mid)
        return 0

    lax.fori_loop(0, NXL, response, 0)

    def chunk(i, _):
        s0 = pl.multiple_of(i * CH, CH)
        rows = pl.ds(s0, CH)
        d = wide(cols_ref[rows, DEC : DEC + 1])
        e = wide(0.5 * time_step * cols_ref[rows, RATE : RATE + 1] * cols_ref[rows, NORM2 : NORM2 + 1])

        def fwd(k, f):
            for j in range(BX):
                x = k * BX + j
                f = v_ref[x, rows, :] + d * f
                out_ref[x, rows, :] = out_ref[x, rows, :] + e * f
            return f

        lax.fori_loop(0, NXL // BX, fwd, jnp.zeros((CH, NYL), F32))

        def bwd(k, g):
            for j in range(BX):
                x = NXL - 1 - (k * BX + j)
                g = d * g
                out_ref[x, rows, :] = out_ref[x, rows, :] + e * g
                g = g + v_ref[x, rows, :]
            return g

        lax.fori_loop(0, NXL // BX, bwd, jnp.zeros((CH, NYL), F32))
        return 0

    lax.fori_loop(0, S // CH, chunk, 0)


def final_kernel(o_ref, rx_ref, cols_ref, out_hbm, cf_ref, cb_ref, buf, sems):
    cols = cols_ref[...]
    lam = col(cols, LAM)
    e = 0.5 * time_step * col(cols, RATE) * col(cols, NORM2)
    cf, cb = read_carries(rx_ref, lax.axis_index("gx"), 8)
    cf_ref[...] = cf * (e * col(cols, DEC))
    cb_ref[...] = cb * (e * jnp.exp(-32.0 * lam))
    copies = []
    for x0 in range(0, NXL, BX):
        for s0 in range(0, S, CH):
            rows = pl.ds(s0, CH)
            d = wide(cols_ref[rows, DEC : DEC + 1])
            inv_d = wide(jnp.exp(cols_ref[rows, LAM : LAM + 1]))
            f, g = cf_ref[rows, :], cb_ref[rows, :]
            for x in range(x0, x0 + BX):
                buf[x, rows, :] = o_ref[x, rows, :] + f + g
                f = f * d
                g = g * inv_d
            cf_ref[rows, :] = f
            cb_ref[rows, :] = g
        for x in range(x0, x0 + BX):
            copy = pltpu.make_async_copy(buf.at[x], out_hbm.at[:, x, :], sems.at[x])
            copy.start()
            copies.append(copy)
    for copy in copies:
        copy.wait()


VM = pl.BlockSpec(memory_space=pltpu.VMEM)
ANY = pl.BlockSpec(memory_space=pl.ANY)
FIELD = (NXL, S, NYL)


def call(kernel, in_specs, outs, out_specs, scratch, microseconds):
    cost = pl.CostEstimate(flops=int(microseconds * 1e9), bytes_accessed=int(microseconds * 2e6), transcendentals=0)
    return pl.pallas_call(
        kernel,
        out_shape=[jax.ShapeDtypeStruct(shape, F32) for shape in outs],
        in_specs=in_specs,
        out_specs=out_specs,
        scratch_shapes=scratch,
        cost_estimate=cost,
        compiler_params=pltpu.CompilerParams(vmem_limit_bytes=VMEM_LIMIT),
    )


def shards(biomass, capacity, adjacency, trophic_level, attack, disp_rate, disp_len):
    inverse = 1.0 / disp_len
    decay = jnp.exp(-inverse)
    norm = (1.0 - decay) / (1.0 + decay)
    basal = (trophic_level == 0).astype(F32)
    level = trophic_level.astype(F32)
    cols = jnp.stack([inverse, decay, norm * norm, disp_rate, attack, basal, level, level], axis=1)

    field = pltpu.VMEM(FIELD, F32)
    plane = pltpu.VMEM((S, NYL), F32)
    dma = pltpu.SemaphoreType.DMA((NXL,))

    (msg,) = call(tails_kernel, [ANY, VM], [(8, S, NYL)], [VM], [field, plane, plane, dma], 3)(biomass, cols)
    rx = lax.all_to_all(msg, "gx", 0, 0)
    q, u, fun = call(
        first_kernel, [ANY, VM, VM, VM], [FIELD, FIELD, (S, NYL)], [VM, VM, VM], [field, dma], 12
    )(biomass, adjacency, capacity, cols)
    car, own, msg = call(
        rows_kernel, [VM, VM, VM], [(2, S, NYL), (S, NYL), (16, S // 2, NYL)], [VM, VM, VM], [], 1
    )(rx, fun, cols)
    ry = lax.all_to_all(msg, "gy", 0, 0)
    mid, p, tail = call(
        local_kernel, [VM, VM, VM, VM], [FIELD, FIELD, (2, S, NYL)], [VM, VM, VM], [plane, plane], 12
    )(u, q, car, cols)
    coef, msg = call(
        columns_kernel, [VM, VM, VM, VM], [(S, NYL), (8, S, NYL)], [VM, VM], [], 1
    )(ry, own, tail, cols)
    rx = lax.all_to_all(msg, "gx", 0, 0)
    (part,) = call(
        second_kernel, [ANY, VM, VM, VM, VM, VM, VM], [FIELD], [VM], [field, field, plane, dma], 12
    )(biomass, adjacency, capacity, cols, mid, p, coef)
    (out,) = call(
        final_kernel, [VM, VM, VM], [(S, NXL, NYL)], [ANY], [plane, plane, field, dma], 3
    )(part, rx, cols)
    return out


def solution(mesh):
    return jax.shard_map(
        shards,
        mesh=mesh,
        in_specs=(P(None, "gx", "gy"), P("gx", "gy"), P(), P(), P(), P(), P()),
        out_specs=P(None, "gx", "gy"),
        check_vma=False,
    )
```

time: 1000 us -> 121 us (0.12)
  the two profiles are of different devices: /device:TPU:22 before, /device:TPU:1 now
where the time goes in v1:
time: 121 us; the launch traced here: 120 us
  Pallas kernels  93.9 us (78%)
  starting transfers between devices  19.3 us (16%)
  local copies, waits for them, and re-layouts  4.4 us (4%)
  other arithmetic  2.05 us (2%)
    pallas_call x1, Pallas kernels, shards(): call(second_kernel, [ANY, VM, VM, VM, VM, VM, VM], [FIELD], [VM], [field,...  28.7 us
    pallas_call x1, Pallas kernels, shards(): call(first_kernel, [ANY, VM, VM, VM], [FIELD, FIELD, (S, NYL)], [VM, VM,...  27.7 us
    pallas_call x1, Pallas kernels, shards(): call(local_kernel, [VM, VM, VM, VM], [FIELD, FIELD, (2, S, NYL)], [VM, VM...  19.3 us
    all_to_all x2, starting transfers between devices, shards(): rx = lax.all_to_all(msg, 'gx', 0, 0)  10.7 us
    all_to_all x1, starting transfers between devices, shards(): ry = lax.all_to_all(msg, 'gy', 0, 0)  8.62 us
    pallas_call x1, Pallas kernels, shards(): call(final_kernel, [VM, VM, VM], [(S, NXL, NYL)], [ANY], [plane, plane, f...  5.39 us
    pallas_call x1, Pallas kernels, shards(): call(tails_kernel, [ANY, VM], [(8, S, NYL)], [VM], [field, plane, plane,...  5.38 us
    pallas_call x1, Pallas kernels, shards(): call(rows_kernel, [VM, VM, VM], [(2, S, NYL), (S, NYL), (16, S // 2, NYL)...  3.76 us
  transfers between devices with their start and end apart: 3, of which 0 were waited for; matrix products, arithmetic and copies ran while one was open for 0% of the time, Pallas kernels for 63%

profile of v1, /device:TPU:1, one launch (start us, length us, event | category | flops | bytes accessed | tf_op | source)
XLA Modules:
  0.0 119.7 jit_solution(2476139819376330345)
XLA Ops:
  0.0 0.7 convert_element_type.4
  0.7 0.7 compare_convert_fusion
  1.4 0.7 divide_multiply_fusion
  2.1 0.7 stack.36
  2.8 0.8 copy.21.cols_ref
  3.6 5.4 %shard_map.74 = f32[8,256,128]{2,1,0:T(8,128)} custom-call(f32[256,32,128]{2,1,0:T(8,128)} %b_hbm.5, f32[256,8]{1,0:T(8,128)} %copy.21.cols_ref), custom_call_target="tpu_custom_call" | custom-call | flops 3000000000 | bytes 6000000 | tf_op jit(solution)/shard_map/pallas_call | solution.py:442
  9.0 5.9 %all-to-all-start = ((f32[8,256,128]{2,1,0:T(8,128)}), f32[8,256,128]{2,1,0:T(8,128)S(1)}, u32[]{:S(2)}, u32[]{:S(2)}) async-start(f32[8,256,128]{2,1,0:T(8,128)} %shard_map.74), calls=%async_computation | async-start | bytes 2097152 | tf_op jit(solution)/shard_map/all_to_all | solution.py:443
  14.8 27.7 %shard_map.73 = (f32[32,256,128]{2,1,0:T(8,128)}, f32[32,256,128]{2,1,0:T(8,128)}, f32[256,128]{1,0:T(8,128)}) custom-call(f32[256,32,128]{2,1,0:T(8,128)} %b_hbm.5, s32[256,256]{1,0:T(8,128)} %adj_ref.3, f32[32,128]{1,0:T(8,128)} %cap_ref.3, f32[256,8]{1,0:T(8,128)} %copy.21.cols_ref), custom_call_target="tpu_custom_call" | custom-call | flops 12000000000 | bytes 24000000 | tf_op jit(solution)/shard_map/pallas_call | solution.py:444
  42.5 0.0 all-to-all-done.rx_ref
  42.5 0.0 copy-start.1
  42.5 1.0 copy-done.1
  43.5 3.8 %shard_map.75 = (f32[2,256,128]{2,1,0:T(8,128)}, f32[256,128]{1,0:T(8,128)}, f32[16,128,128]{2,1,0:T(8,128)}) custom-call(f32[8,256,128]{2,1,0:T(8,128)} %copy-done.1, f32[256,128]{1,0:T(8,128)} %get-tuple-element.18.fun_ref, f32[256,8]{1,0:T(8,128)} %copy.21.cols_ref), custom_call_target="tpu_custom_call" | custom-call | flops 1000000000 | bytes 2000000 | tf_op jit(solution)/shard_map/pallas_call | solution.py:447
  47.3 8.6 %all-to-all-start.1 = ((f32[16,128,128]{2,1,0:T(8,128)}), f32[16,128,128]{2,1,0:T(8,128)S(1)}, u32[]{:S(2)}, u32[]{:S(2)}) async-start(f32[16,128,128]{2,1,0:T(8,128)} %get-tuple-element.22), calls=%async_computation.1 | async-start | bytes 2097152 | tf_op jit(solution)/shard_map/all_to_all | solution.py:450
  55.9 19.3 %shard_map.76 = (f32[32,256,128]{2,1,0:T(8,128)}, f32[32,256,128]{2,1,0:T(8,128)}, f32[2,256,128]{2,1,0:T(8,128)}) custom-call(f32[32,256,128]{2,1,0:T(8,128)} %get-tuple-element.16.u_ref, f32[32,256,128]{2,1,0:T(8,128)} %get-tuple-element.17.q_ref, f32[2,256,128]{2,1,0:T(8,128)} %get-tuple-element.19.car_ref, f32[256,8]{1,0:T(8,128)} %copy.21.cols_ref), custom_call_target="tpu_custom_call" | custom-call | flops 12000000000 | bytes 24000000 | tf_op jit(solution)/shard_map/pallas_call | solution.py:451
  75.2 0.0 all-to-all-done.1.ry_ref
  75.2 0.0 copy-start
  75.2 1.0 copy-done
  76.1 3.7 %shard_map.77 = (f32[256,128]{1,0:T(8,128)}, f32[8,256,128]{2,1,0:T(8,128)}) custom-call(f32[16,128,128]{2,1,0:T(8,128)} %copy-done, f32[256,128]{1,0:T(8,128)} %get-tuple-element.23.own_ref, f32[2,256,128]{2,1,0:T(8,128)} %get-tuple-element.24.tail_ref, f32[256,8]{1,0:T(8,128)} %copy.21.cols_ref), custom_call_target="tpu_custom_call" | custom-call | flops 1000000000 | bytes 2000000 | tf_op jit(solution)/shard_map/pallas_call | solution.py:454
  79.8 4.8 %all-to-all-start.2 = ((f32[8,256,128]{2,1,0:T(8,128)}), f32[8,256,128]{2,1,0:T(8,128)S(1)}, u32[]{:S(2)}, u32[]{:S(2)}) async-start(f32[8,256,128]{2,1,0:T(8,128)} %get-tuple-element.26), calls=%async_computation.2 | async-start | bytes 2097152 | tf_op jit(solution)/shard_map/all_to_all | solution.py:457
  84.7 28.7 %shard_map.78.o_ref = f32[32,256,128]{2,1,0:T(8,128)} custom-call(f32[256,32,128]{2,1,0:T(8,128)} %b_hbm.5, s32[256,256]{1,0:T(8,128)} %adj_ref.3, f32[32,128]{1,0:T(8,128)} %cap_ref.3, f32[256,8]{1,0:T(8,128)} %copy.21.cols_ref, f32[32,256,128]{2,1,0:T(8,128)} %get-tuple-element.20.mid_ref, f32[32,256,128]{2,1,0:T(8,128)} %get-tuple-element.21.p_ref, ...), custom_call_target="tpu_custom_call" | custom-call | flops 12000000000 | bytes 24000000 | tf_op jit(solution)/shard_map/pallas_call | solution.py:458
  113.4 0.0 all-to-all-done.2.rx_ref
  113.4 0.0 copy-start.2
  113.4 1.0 copy-done.2
  114.3 5.4 %shard_map.79 = f32[256,32,128]{2,1,0:T(8,128)} custom-call(f32[32,256,128]{2,1,0:T(8,128)} %shard_map.78.o_ref, f32[8,256,128]{2,1,0:T(8,128)} %copy-done.2, f32[256,8]{1,0:T(8,128)} %copy.21.cols_ref), custom_call_target="tpu_custom_call" | custom-call | flops 3000000000 | bytes 6000000 | tf_op jit(solution)/shard_map/pallas_call | solution.py:461
  (1 shorter events, 0.0 us)
Async XLA Ops:
  9.0 33.6 %all-to-all-start = ((f32[8,256,128]{2,1,0:T(8,128)}), f32[8,256,128]{2,1,0:T(8,128)S(1)}, u32[]{:S(2)}, u32[]{:S(2)}) async-start(f32[8,256,128]{2,1,0:T(8,128)} %shard_map.74), calls=%async_computation | async-start | bytes 2097152 | tf_op jit(solution)/shard_map/all_to_all | solution.py:443
  42.5 1.0 copy-start.1
  47.3 27.9 %all-to-all-start.1 = ((f32[16,128,128]{2,1,0:T(8,128)}), f32[16,128,128]{2,1,0:T(8,128)S(1)}, u32[]{:S(2)}, u32[]{:S(2)}) async-start(f32[16,128,128]{2,1,0:T(8,128)} %get-tuple-element.22), calls=%async_computation.1 | async-start | bytes 2097152 | tf_op jit(solution)/shard_map/all_to_all | solution.py:450
  75.2 1.0 copy-start
  79.8 33.5 %all-to-all-start.2 = ((f32[8,256,128]{2,1,0:T(8,128)}), f32[8,256,128]{2,1,0:T(8,128)S(1)}, u32[]{:S(2)}, u32[]{:S(2)}) async-start(f32[8,256,128]{2,1,0:T(8,128)} %get-tuple-element.26), calls=%async_computation.2 | async-start | bytes 2097152 | tf_op jit(solution)/shard_map/all_to_all | solution.py:457
  113.4 1.0 copy-start.2

commit v2 on v0

v2 whole, which is shorter than its diff:
```python
import jax
import jax.numpy as jnp
from jax import lax
from jax.experimental import pallas as pl
from jax.experimental.pallas import tpu as pltpu
from jax.sharding import PartitionSpec as P

time_step = 0.25
handling = 1.0
efficiency = 0.6
mortal_rate = 0.15

S = 256
NXL = 32
NYL = 128
CH = 64
BX = 8
BR = 4
BL = 4
F32 = jnp.float32
BF16 = jnp.bfloat16
VMEM_LIMIT = 32 * 1024 * 1024


LAM, DEC, NORM2, RATE, ATT, BASAL, LEVEL = range(7)
HOP_X, HOP_Y, WF, FH, WB, BH, UP, DOWN, TURN, RUN = range(10)
GROUPS = (BH, WB, FH, WF)


def col(cols, k):
    return cols[:, k : k + 1]


def lanes(rows):
    return lax.broadcasted_iota(jnp.int32, (rows, NYL), 1)


def wide(column):
    return jnp.broadcast_to(column, (column.shape[0], NYL))


def lane_sum(v):
    return jnp.sum(v, axis=1, keepdims=True)


def split(v):
    hi = v.astype(BF16)
    lo = (v - hi.astype(F32)).astype(BF16)
    return jnp.concatenate([hi, lo], axis=1)


def triangles():
    i = lax.broadcasted_iota(jnp.int32, (2 * NYL, NYL), 0) % NYL
    j = lax.broadcasted_iota(jnp.int32, (2 * NYL, NYL), 1)
    return (i <= j).astype(F32).astype(BF16), (i > j).astype(F32).astype(BF16)


def smooth_rows(v, a, ia, low, upp):
    f = jnp.dot(split(v * ia), low, preferred_element_type=F32)
    g = jnp.dot(split(v * a), upp, preferred_element_type=F32)
    return f * a + g * ia


def respond(v, rcap, adj, adj_t, att, basal, level):
    p = jnp.maximum(v, 0.0)
    both = jnp.dot(adj_t, split(p), preferred_element_type=F32)
    grazing = att * (both[:, :NYL] + both[:, NYL:])
    handled = p / (1.0 + handling * grazing)
    back = jnp.dot(adj, split(att * handled), preferred_element_type=F32)
    loss = back[:, :NYL] + back[:, NYL:]
    return p * (basal - mortal_rate * level - basal * p * rcap - loss) + efficiency * handled * grazing


def food_web(adj_ref, cols):
    adj = adj_ref[...].astype(F32)
    return (adj.astype(BF16), adj.T.astype(BF16)) + tuple(wide(col(cols, k)) for k in (ATT, BASAL, LEVEL))


def read_carries(rx_ref, hop, me, count):
    cf = jnp.zeros(rx_ref.shape[1:], F32)
    cb = jnp.zeros(rx_ref.shape[1:], F32)
    for k in range(count):
        cf = jnp.where(k < me, rx_ref[k] + hop * cf, cf)
    for k in range(count - 1, -1, -1):
        cb = jnp.where(k > me, rx_ref[k] + hop * cb, cb)
    return cf, cb


def write_messages(msg_ref, front, back, me, count):
    for k in range(count):
        msg_ref[k] = jnp.where(k > me, front, back)


def column_in(b_hbm, buf, sems, x):
    return pltpu.make_async_copy(b_hbm.at[:, x, :], buf.at[x], sems.at[x])


def plane_in(hbm, buf, sems, x):
    return pltpu.make_async_copy(hbm.at[x], buf.at[x], sems.at[x])


def plane_out(buf, hbm, sems, x):
    return pltpu.make_async_copy(buf.at[x], hbm.at[x], sems.at[x])


def chunk_out(buf, hbm, sems, i):
    part = pl.ds(pl.multiple_of(i * CH, CH), CH)
    return pltpu.make_async_copy(buf.at[:, part, :], hbm.at[:, part, :], sems.at[i])


def each(first, last, act):
    def body(k, _):
        act(k)
        return 0

    lax.fori_loop(first, last, body, 0)


def tails_kernel(b_hbm, level_hbm, attack_hbm, rate_hbm, length_hbm, cols_ref, msg_ref, bt, level, vec, fr, ba, sems, vsems):
    sources = (length_hbm, rate_hbm, attack_hbm)
    small = [pltpu.make_async_copy(h, vec.at[pl.ds(k, 1), :], vsems.at[k]) for k, h in enumerate(sources)]
    small.append(pltpu.make_async_copy(level_hbm, level, vsems.at[3]))
    for copy in small:
        copy.start()
    copies = [column_in(b_hbm, bt, sems, x) for x in range(NXL)]
    for copy in copies:
        copy.start()
    for copy in small:
        copy.wait()
    me = lax.axis_index("gx")
    lam = 1.0 / vec[0:1, :]
    dec = jnp.exp(-lam)
    norm = (1.0 - dec) / (1.0 + dec)
    basal = (level[...] == 0).astype(F32)
    rows = [lam, dec, norm * norm, vec[1:2, :], vec[2:3, :], basal, level[...].astype(F32)]
    cols_ref[...] = jnp.concatenate(rows + [jnp.zeros((NYL - len(rows), S), F32)], axis=0).T
    for x0 in range(0, NXL, BX):
        for x in range(x0, x0 + BX):
            copies[x].wait()
        for s0 in range(0, S, CH):
            part = pl.ds(s0, CH)
            d = wide(cols_ref[part, DEC : DEC + 1])
            vs = [bt[x, part, :] for x in range(x0, x0 + BX)]
            f = fr[part, :] if x0 else jnp.zeros((CH, NYL), F32)
            for v in vs:
                f = v + d * f
            g = vs[-1]
            for v in vs[-2::-1]:
                g = v + d * g
            if x0:
                g = ba[part, :] + wide(jnp.exp(-float(x0) * cols_ref[part, LAM : LAM + 1])) * g
            fr[part, :] = f
            ba[part, :] = g
    write_messages(msg_ref, fr[...], ba[...], me, 8)


def by_group(lane, parts):
    out = parts[3]
    for k in (2, 1, 0):
        out = jnp.where(lane < 32 * (k + 1), parts[k], out)
    return out


def fill_tables(tab_ref, cols, my):
    lam, dec = col(cols, LAM), col(cols, DEC)
    c = time_step * col(cols, RATE) * col(cols, NORM2)
    lane = lanes(S)
    y = lane.astype(F32)
    xl = (lane % 32).astype(F32)
    inv = 1.0 / ((1.0 - dec) * (1.0 + dec))
    wf = jnp.exp(-lam * (127.0 - y))
    wb = jnp.exp(-lam * y)
    tab_ref[HOP_X] = wide(jnp.exp(-32.0 * lam))
    tab_ref[HOP_Y] = wide(jnp.exp(-128.0 * lam))
    tab_ref[WF] = wf
    tab_ref[WB] = wb
    tab_ref[FH] = c * ((128.0 - y) * wf + (jnp.exp(-lam * (129.0 - y)) - jnp.exp(-lam * (129.0 + y))) * inv)
    tab_ref[BH] = c * ((y + 1.0) * wb + (jnp.exp(-lam * (y + 2.0)) - jnp.exp(-lam * (256.0 - y))) * inv)
    tab_ref[UP] = jnp.exp(-lam * (xl + 1.0))
    tab_ref[DOWN] = jnp.exp(-lam * (32.0 - xl))
    below, above = my.astype(F32), (15 - my).astype(F32)
    scale = c * dec * inv
    zero = jnp.zeros((S, 1), F32)
    tb = scale * (1.0 - jnp.exp(-256.0 * below * lam))
    ta = scale * (1.0 - jnp.exp(-256.0 * above * lam))
    tab_ref[TURN] = by_group(lane, [zero, tb, zero, ta])
    run = 128.0 * c
    tab_ref[RUN] = by_group(lane, [zero, run, zero, run])


def first_kernel(
    b_hbm, adj_ref, cap_ref, cols_ref, q_hbm, u_hbm, fun_ref, tab_ref, bt_ref, q_ref, u_ref, b_sems, q_sems, u_sems
):
    each(0, NXL, lambda x: column_in(b_hbm, bt_ref, b_sems, x).start())
    cols = cols_ref[...]
    fill_tables(tab_ref, cols, lax.axis_index("gy"))
    web = food_web(adj_ref, cols)
    rate = wide(col(cols, RATE))

    def response(i, _):
        for j in range(BR):
            x = i * BR + j
            column_in(b_hbm, bt_ref, b_sems, x).wait()
        for j in range(BR):
            x = i * BR + j
            v = bt_ref[x]
            rcap = 1.0 / cap_ref[pl.ds(x, 1), :]
            q_ref[x] = v + time_step * (respond(v, rcap, *web) - rate * v)
        for j in range(BR):
            plane_out(q_ref, q_hbm, q_sems, i * BR + j).start()
        return 0

    lax.fori_loop(0, NXL // BR, response, 0)

    def chunk(i, _):
        part = pl.ds(pl.multiple_of(i * CH, CH), CH)
        d = wide(cols_ref[part, DEC : DEC + 1])
        wf, hf, wb, hb = (tab_ref[k, part, :] for k in (WF, FH, WB, BH))
        lane = lanes(CH)

        def fwd(k, f):
            for j in range(BX):
                x = k * BX + j
                f = bt_ref[x, part, :] + d * f
                u_ref[x, part, :] = f
            return f

        lax.fori_loop(0, NXL // BX, fwd, jnp.zeros((CH, NYL), F32))

        def bwd(k, carry):
            g, acc = carry
            for j in range(BX):
                x = NXL - 1 - (k * BX + j)
                g = d * g
                u = u_ref[x, part, :] + g
                u_ref[x, part, :] = u
                g = g + bt_ref[x, part, :]
                q = q_ref[x, part, :]
                acc = jnp.where(lane == x, lane_sum(wf * u), acc)
                acc = jnp.where(lane == x + 32, lane_sum(wf * q + hf * u), acc)
                acc = jnp.where(lane == x + 64, lane_sum(wb * u), acc)
                acc = jnp.where(lane == x + 96, lane_sum(wb * q + hb * u), acc)
            return g, acc

        zero = jnp.zeros((CH, NYL), F32)
        fun_ref[part, :] = lax.fori_loop(0, NXL // BX, bwd, (zero, zero))[1]
        chunk_out(u_ref, u_hbm, u_sems, i).start()
        return 0

    lax.fori_loop(0, S // CH, chunk, 0)
    each(0, NXL, lambda x: plane_out(q_ref, q_hbm, q_sems, x).wait())
    each(0, S // CH, lambda i: chunk_out(u_ref, u_hbm, u_sems, i).wait())


def rows_kernel(rx_ref, fun_ref, tab_ref, car_ref, own_ref, msg_ref):
    mx, my = lax.axis_index("gx"), lax.axis_index("gy")
    cf, cb = read_carries(rx_ref, tab_ref[HOP_X], mx, 8)
    car_ref[0] = cf
    car_ref[1] = cb
    lane = lanes(S)
    pf = by_group(lane, [lane_sum(tab_ref[k] * cf) for k in (WF, FH, WB, BH)])
    pb = by_group(lane, [lane_sum(tab_ref[k] * cb) for k in (WF, FH, WB, BH)])
    fun = fun_ref[...] + tab_ref[UP] * pf + tab_ref[DOWN] * pb
    own_ref[...] = fun
    fun = fun + tab_ref[TURN] * tab_ref[HOP_Y] * pltpu.roll(fun, 96, 1)
    half = S // 2
    low_lanes = lanes(half) < 64
    front = jnp.where(low_lanes, fun[:half], pltpu.roll(fun[half:], 64, 1))
    back = jnp.where(low_lanes, pltpu.roll(fun[:half], 64, 1), fun[half:])
    write_messages(msg_ref, front, back, my, 16)


def local_kernel(
    u_hbm, q_hbm, car_ref, cols_ref, mid_hbm, p_hbm, tail_ref, u_ref, q_ref, up_ref, down_ref, u_sems, q_sems, p_sems, m_sems
):
    def fetch(x):
        plane_in(u_hbm, u_ref, u_sems, x).start()
        plane_in(q_hbm, q_ref, q_sems, x).start()

    each(0, NXL, fetch)
    cols = cols_ref[...]
    lam = col(cols, LAM)
    c = wide(time_step * col(cols, RATE) * col(cols, NORM2))
    d = wide(col(cols, DEC))
    inv_d = wide(jnp.exp(lam))
    y = lanes(S).astype(F32) - 64.0
    a, ia = jnp.exp(-lam * y), jnp.exp(lam * y)
    low, upp = triangles()
    tail_ref[...] = jnp.zeros_like(tail_ref)
    up_ref[...] = d
    down_ref[...] = wide(jnp.exp(-32.0 * lam))

    def step(i, _):
        for j in range(BL):
            plane_in(u_hbm, u_ref, u_sems, i * BL + j).wait()
            plane_in(q_hbm, q_ref, q_sems, i * BL + j).wait()
        for j in range(BL):
            x = i * BL + j
            up, down = up_ref[...], down_ref[...]
            u = u_ref[x] + up * car_ref[0] + down * car_ref[1]
            mid = q_ref[x] + c * smooth_rows(u, a, ia, low, upp)
            q_ref[x] = mid
            p = smooth_rows(mid, a, ia, low, upp)
            u_ref[x] = p
            tail_ref[0] = p + d * tail_ref[0]
            tail_ref[1] = tail_ref[1] + up * inv_d * p
            up_ref[...] = up * d
            down_ref[...] = down * inv_d
        for j in range(BL):
            plane_out(q_ref, mid_hbm, m_sems, i * BL + j).start()
            plane_out(u_ref, p_hbm, p_sems, i * BL + j).start()
        return 0

    lax.fori_loop(0, NXL // BL, step, 0)

    def drain(x):
        plane_out(q_ref, mid_hbm, m_sems, x).wait()
        plane_out(u_ref, p_hbm, p_sems, x).wait()

    each(0, NXL, drain)


def columns_kernel(ry_ref, own_ref, tail_ref, tab_ref, coef_ref, msg_ref):
    mx, my = lax.axis_index("gx"), lax.axis_index("gy")
    half = S // 2
    low_lanes = lanes(half) < 64
    hop = jnp.where(low_lanes, tab_ref[HOP_Y, :half, :], tab_ref[HOP_Y, half:, :])
    zero = jnp.zeros((half, NYL), F32)
    lo, lo2, hi, hi2 = zero, zero, zero, zero
    for k in range(15):
        lo2 = jnp.where(k < my, hop * (lo2 + lo), lo2)
        lo = jnp.where(k < my, ry_ref[k] + hop * lo, lo)
    for k in range(15, 0, -1):
        hi2 = jnp.where(k > my, hop * (hi2 + hi), hi2)
        hi = jnp.where(k > my, ry_ref[k] + hop * hi, hi)

    def unpack(low, high):
        top = jnp.where(low_lanes, low, pltpu.roll(high, 64, 1))
        bottom = jnp.where(low_lanes, pltpu.roll(low, 64, 1), high)
        return jnp.concatenate([top, bottom], axis=0)

    coef = unpack(lo, hi) + tab_ref[RUN] * pltpu.roll(unpack(lo2, hi2), 32, 1)
    coef = coef + tab_ref[TURN] * pltpu.roll(own_ref[...] + tab_ref[HOP_Y] * coef, 96, 1)
    coef_ref[...] = coef
    lane = lanes(S)
    at_front, at_back = coef * tab_ref[DOWN], coef * tab_ref[UP]
    front, back = tail_ref[0], tail_ref[1]
    for k, table in enumerate(GROUPS):
        inside = (lane >= 32 * k) & (lane < 32 * (k + 1))
        weight = tab_ref[table]
        front = front + lane_sum(jnp.where(inside, at_front, 0.0)) * weight
        back = back + lane_sum(jnp.where(inside, at_back, 0.0)) * weight
    write_messages(msg_ref, front, back, mx, 8)


def second_kernel(
    b_hbm, adj_ref, cap_ref, cols_ref, tab_ref, mid_hbm, p_hbm, coef_ref, out_hbm,
    out_ref, mid_ref, v_ref, roll_ref, b_sems, m_sems, p_sems, o_sems,
):
    def fetch(x):
        column_in(b_hbm, out_ref, b_sems, x).start()
        plane_in(mid_hbm, mid_ref, m_sems, x).start()
        plane_in(p_hbm, v_ref, p_sems, x).start()

    each(0, NXL, fetch)
    cols = cols_ref[...]
    web = food_web(adj_ref, cols)
    rate, d = wide(col(cols, RATE)), wide(col(cols, DEC))
    c = wide(time_step * col(cols, RATE) * col(cols, NORM2))
    ef, eb, alpha, beta = (d * tab_ref[k] for k in (WB, WF, BH, FH))
    roll_ref[...] = coef_ref[...]

    def response(i, _):
        for j in range(BR):
            x = i * BR + j
            column_in(b_hbm, out_ref, b_sems, x).wait()
            plane_in(mid_hbm, mid_ref, m_sems, x).wait()
            plane_in(p_hbm, v_ref, p_sems, x).wait()
        for j in range(BR):
            x = i * BR + j
            coef = roll_ref[...]
            cfu, cfm, cbu, cbm = (coef[:, 32 * k : 32 * k + 1] for k in range(4))
            roll_ref[...] = pltpu.roll(coef, 127, 1)
            mid = mid_ref[x] + c * (cfu * ef + cbu * eb)
            v_ref[x] = v_ref[x] + cfu * alpha + cbu * beta + cfm * ef + cbm * eb
            rcap = 1.0 / cap_ref[pl.ds(x, 1), :]
            r = respond(mid, rcap, *web)
            out_ref[x] = 0.5 * (out_ref[x] + mid) + 0.5 * time_step * (r - rate * mid)
        return 0

    lax.fori_loop(0, NXL // BR, response, 0)

    def chunk(i, _):
        part = pl.ds(pl.multiple_of(i * CH, CH), CH)
        d = wide(cols_ref[part, DEC : DEC + 1])
        e = wide(0.5 * time_step * cols_ref[part, RATE : RATE + 1] * cols_ref[part, NORM2 : NORM2 + 1])

        def fwd(k, f):
            for j in range(BX):
                x = k * BX + j
                f = v_ref[x, part, :] + d * f
                out_ref[x, part, :] = out_ref[x, part, :] + e * f
            return f

        lax.fori_loop(0, NXL // BX, fwd, jnp.zeros((CH, NYL), F32))

        def bwd(k, g):
            for j in range(BX):
                x = NXL - 1 - (k * BX + j)
                g = d * g
                out_ref[x, part, :] = out_ref[x, part, :] + e * g
                g = g + v_ref[x, part, :]
            return g

        lax.fori_loop(0, NXL // BX, bwd, jnp.zeros((CH, NYL), F32))
        chunk_out(out_ref, out_hbm, o_sems, i).start()
        return 0

    lax.fori_loop(0, S // CH, chunk, 0)
    each(0, S // CH, lambda i: chunk_out(out_ref, out_hbm, o_sems, i).wait())


def final_kernel(o_hbm, rx_ref, cols_ref, tab_ref, out_hbm, cf_ref, cb_ref, buf, in_sems, sems):
    loads = [plane_in(o_hbm, buf, in_sems, x) for x in range(NXL)]
    for copy in loads:
        copy.start()
    cols = cols_ref[...]
    lam = col(cols, LAM)
    e = 0.5 * time_step * col(cols, RATE) * col(cols, NORM2)
    cf, cb = read_carries(rx_ref, tab_ref[HOP_X], lax.axis_index("gx"), 8)
    cf_ref[...] = cf * (e * col(cols, DEC))
    cb_ref[...] = cb * (e * jnp.exp(-32.0 * lam))
    copies = [pltpu.make_async_copy(buf.at[x], out_hbm.at[:, x, :], sems.at[x]) for x in range(NXL)]
    for x0 in range(0, NXL, BX):
        for x in range(x0, x0 + BX):
            loads[x].wait()
        for s0 in range(0, S, CH):
            part = pl.ds(s0, CH)
            d = wide(cols_ref[part, DEC : DEC + 1])
            inv_d = wide(jnp.exp(cols_ref[part, LAM : LAM + 1]))
            f, g = cf_ref[part, :], cb_ref[part, :]
            for x in range(x0, x0 + BX):
                buf[x, part, :] = buf[x, part, :] + f + g
                f = f * d
                g = g * inv_d
            cf_ref[part, :] = f
            cb_ref[part, :] = g
        for x in range(x0, x0 + BX):
            copies[x].start()
    for copy in copies:
        copy.wait()


VM = pl.BlockSpec(memory_space=pltpu.VMEM)
HBM = pl.BlockSpec(memory_space=pltpu.HBM)
FIELD = (NXL, S, NYL)
PLANE = (S, NYL)


def in_vmem(x):
    return pltpu.with_memory_space_constraint(x, pltpu.VMEM)


def in_hbm(x):
    return pltpu.with_memory_space_constraint(x, pltpu.HBM)


def call(kernel, operands, outs, scratch, microseconds):
    cost = pl.CostEstimate(flops=int(microseconds * 1e9), bytes_accessed=int(microseconds * 2e6), transcendentals=0)
    return pl.pallas_call(
        kernel,
        out_shape=[shape for shape, _ in outs],
        in_specs=[spec for _, spec in operands],
        out_specs=[spec for _, spec in outs],
        scratch_shapes=scratch,
        cost_estimate=cost,
        compiler_params=pltpu.CompilerParams(vmem_limit_bytes=VMEM_LIMIT),
    )(*[in_hbm(x) if spec is HBM else x for x, spec in operands])


def shards(biomass, capacity, adjacency, trophic_level, attack, disp_rate, disp_len):
    field = pltpu.VMEM(FIELD, F32)
    plane = pltpu.VMEM(PLANE, F32)
    columns = pltpu.SemaphoreType.DMA((NXL,))
    chunks = pltpu.SemaphoreType.DMA((S // CH,))
    field_out = (pltpu.HBM(FIELD, F32), HBM)
    plane_out = (plane, VM)
    x_out = (pltpu.HBM((8,) + PLANE, F32), VM)
    y_out = (pltpu.HBM((16, S // 2, NYL), F32), VM)
    pair_out = (pltpu.VMEM((2,) + PLANE, F32), VM)
    tables_out = (pltpu.VMEM((10,) + PLANE, F32), VM)
    result = (pltpu.HBM((S, NXL, NYL), F32), HBM)

    vectors = [(v.reshape(1, S), HBM) for v in (trophic_level, attack, disp_rate, disp_len)]
    b = (biomass, HBM)
    adj, cap = (adjacency, VM), (capacity, VM)
    cols, msg = call(
        tails_kernel,
        [b] + vectors,
        [plane_out, x_out],
        [field, pltpu.VMEM((1, S), jnp.int32), pltpu.VMEM((8, S), F32), plane, plane, columns, pltpu.SemaphoreType.DMA((4,))],
        3,
    )
    cols = (in_vmem(cols), VM)
    rx = in_vmem(lax.all_to_all(msg, "gx", 0, 0))
    q, u, fun, tab = call(
        first_kernel,
        [b, adj, cap, cols],
        [field_out, field_out, plane_out, tables_out],
        [field, field, field, columns, columns, chunks],
        12,
    )
    tab = (in_vmem(tab), VM)
    car, own, msg = call(
        rows_kernel, [(rx, VM), (in_vmem(fun), VM), tab], [pair_out, plane_out, y_out], [], 1
    )
    ry = in_vmem(lax.all_to_all(msg, "gy", 0, 0))
    mid, p, tail = call(
        local_kernel,
        [(u, HBM), (q, HBM), (in_vmem(car), VM), cols],
        [field_out, field_out, pair_out],
        [field, field, plane, plane, columns, columns, columns, columns],
        12,
    )
    coef, msg = call(
        columns_kernel, [(ry, VM), (in_vmem(own), VM), (in_vmem(tail), VM), tab], [plane_out, x_out], [], 1
    )
    rx = in_vmem(lax.all_to_all(msg, "gx", 0, 0))
    (part,) = call(
        second_kernel,
        [b, adj, cap, cols, tab, (mid, HBM), (p, HBM), (in_vmem(coef), VM)],
        [field_out],
        [field, field, field, plane, columns, columns, columns, chunks],
        12,
    )
    (out,) = call(
        final_kernel, [(part, HBM), (rx, VM), cols, tab], [result], [plane, plane, field, columns, columns], 3
    )
    return out


def solution(mesh):
    return jax.shard_map(
        shards,
        mesh=mesh,
        in_specs=(P(None, "gx", "gy"), P("gx", "gy"), P(), P(), P(), P(), P()),
        out_specs=P(None, "gx", "gy"),
        check_vma=False,
    )
```

time: 1000 us -> 80.1 us (0.08)
  the two profiles are of different devices: /device:TPU:22 before, /device:TPU:1 now
where the time goes in v2:
time: 80.1 us; the launch traced here: 79.8 us
  Pallas kernels  54.9 us (69%)
  starting transfers between devices  18.7 us (23%)
  waiting for transfers between devices  6.1 us (8%)
    pallas_call x7, Pallas kernels, call(): pl.pallas_call(kernel, out_shape=[shape for shape, _ in outs], in_specs=[...  54.9 us
    all_to_all x2, starting transfers between devices, shards(): rx = in_vmem(lax.all_to_all(msg, 'gx', 0, 0))  9.43 us
    all_to_all x1, starting transfers between devices, shards(): ry = in_vmem(lax.all_to_all(msg, 'gy', 0, 0))  9.29 us
    all_to_all x1, waiting for transfers between devices, shards(): ry = in_vmem(lax.all_to_all(msg, 'gy', 0, 0))  5.19 us
  transfers between devices with their start and end apart: 3, of which 2 were waited for; matrix products, arithmetic and copies ran while one was open for 0% of the time, Pallas kernels for 53%

profile of v2, /device:TPU:1, one launch (start us, length us, event | category | flops | bytes accessed | tf_op | source)
XLA Modules:
  0.0 79.8 jit_solution(9305040985481391481)
XLA Ops:
  0.0 0.0 copy-start
  0.0 0.0 copy-start.1
  0.0 4.9 %shard_map.73 = (f32[256,128]{1,0:T(8,128)S(1)}, f32[8,256,128]{2,1,0:T(8,128)}) custom-call(f32[256,32,128]{2,1,0:T(8,128)} %b_hbm.5, s32[1,256]{1,0:T(1,128)} %bitcast.4, f32[1,256]{1,0:T(1,128)} %bitcast.5, f32[1,256]{1,0:T(1,128)} %bitcast.6, f32[1,256]{1,0:T(1,128)} %bitcast.7), custom_call_target="tpu_custom_call" | custom-call | flops 3000000000 | bytes 6000000 | tf_op jit(solution)/shard_map/pallas_call | solution.py:470
  5.0 5.9 %all-to-all-start = ((f32[8,256,128]{2,1,0:T(8,128)}), f32[8,256,128]{2,1,0:T(8,128)S(1)}, u32[]{:S(2)}, u32[]{:S(2)}) async-start(f32[8,256,128]{2,1,0:T(8,128)} %get-tuple-element.23), calls=%async_computation | async-start | bytes 2097152 | tf_op jit(solution)/shard_map/all_to_all | solution.py:505
  10.8 0.0 copy-done
  10.8 0.0 copy-done.1
  10.8 14.3 %shard_map.74 = (f32[32,256,128]{2,1,0:T(8,128)}, f32[32,256,128]{2,1,0:T(8,128)}, f32[256,128]{1,0:T(8,128)S(1)}, f32[10,256,128]{2,1,0:T(8,128)S(1)}) custom-call(f32[256,32,128]{2,1,0:T(8,128)} %b_hbm.5, s32[256,256]{1,0:T(8,128)S(1)} %copy-done, f32[32,128]{1,0:T(8,128)S(1)} %copy-done.1, f32[256,128]{1,0:T(8,128)S(1)} %get-tuple-element.19.cols_ref), custom_call_target="tpu_custom_call" | custom-call | flops 12000000000 | bytes 24000000 | tf_op jit(solution)/shard_map/pallas_call | solution.py:470
  25.1 0.9 %all-to-all-done.rx_ref = f32[8,256,128]{2,1,0:T(8,128)S(1)} async-done(((f32[8,256,128]{2,1,0:T(8,128)}), f32[8,256,128]{2,1,0:T(8,128)S(1)}, u32[]{:S(2)}, u32[]{:S(2)}) %all-to-all-start) | async-done | bytes 1048608 | tf_op jit(solution)/shard_map/all_to_all | solution.py:505
  26.0 1.8 %shard_map.75 = (f32[2,256,128]{2,1,0:T(8,128)S(1)}, f32[256,128]{1,0:T(8,128)S(1)}, f32[16,128,128]{2,1,0:T(8,128)}) custom-call(f32[8,256,128]{2,1,0:T(8,128)S(1)} %all-to-all-done.rx_ref, f32[256,128]{1,0:T(8,128)S(1)} %get-tuple-element.24.fun_ref, f32[10,256,128]{2,1,0:T(8,128)S(1)} %get-tuple-element.20.tab_ref), custom_call_target="tpu_custom_call" | custom-call | flops 1000000000 | bytes 2000000 | tf_op jit(solution)/shard_map/pallas_call | solution.py:470
  27.8 9.3 %all-to-all-start.1 = ((f32[16,128,128]{2,1,0:T(8,128)}), f32[16,128,128]{2,1,0:T(8,128)S(1)}, u32[]{:S(2)}, u32[]{:S(2)}) async-start(f32[16,128,128]{2,1,0:T(8,128)} %get-tuple-element.28), calls=%async_computation.1 | async-start | bytes 2097152 | tf_op jit(solution)/shard_map/all_to_all | solution.py:517
  37.1 12.0 %shard_map.76 = (f32[32,256,128]{2,1,0:T(8,128)}, f32[32,256,128]{2,1,0:T(8,128)}, f32[2,256,128]{2,1,0:T(8,128)S(1)}) custom-call(f32[32,256,128]{2,1,0:T(8,128)} %get-tuple-element.21.u_hbm, f32[32,256,128]{2,1,0:T(8,128)} %get-tuple-element.22.q_hbm, f32[2,256,128]{2,1,0:T(8,128)S(1)} %get-tuple-element.25.car_ref, f32[256,128]{1,0:T(8,128)S(1)} %get-tuple-element.19.cols_ref), custom_call_target="tpu_custom_call" | custom-call | flops 12000000000 | bytes 24000000 | tf_op jit(solution)/shard_map/pallas_call | solution.py:470
  49.2 5.2 %all-to-all-done.1.ry_ref = f32[16,128,128]{2,1,0:T(8,128)S(1)} async-done(((f32[16,128,128]{2,1,0:T(8,128)}), f32[16,128,128]{2,1,0:T(8,128)S(1)}, u32[]{:S(2)}, u32[]{:S(2)}) %all-to-all-start.1) | async-done | bytes 1048608 | tf_op jit(solution)/shard_map/all_to_all | solution.py:517
  54.3 2.0 %shard_map.77 = (f32[256,128]{1,0:T(8,128)S(1)}, f32[8,256,128]{2,1,0:T(8,128)}) custom-call(f32[16,128,128]{2,1,0:T(8,128)S(1)} %all-to-all-done.1.ry_ref, f32[256,128]{1,0:T(8,128)S(1)} %get-tuple-element.29.own_ref, f32[2,256,128]{2,1,0:T(8,128)S(1)} %get-tuple-element.30.tail_ref, f32[10,256,128]{2,1,0:T(8,128)S(1)} %get-tuple-element.20.tab_ref), custom_call_target="tpu_custom_call" | custom-call | flops 1000000000 | bytes 2000000 | tf_op jit(solution)/shard_map/pallas_call | solution.py:470
  56.3 3.6 %all-to-all-start.2 = ((f32[8,256,128]{2,1,0:T(8,128)}), f32[8,256,128]{2,1,0:T(8,128)S(1)}, u32[]{:S(2)}, u32[]{:S(2)}) async-start(f32[8,256,128]{2,1,0:T(8,128)} %get-tuple-element.32), calls=%async_computation.2 | async-start | bytes 2097152 | tf_op jit(solution)/shard_map/all_to_all | solution.py:528
  59.9 15.7 %shard_map.78.o_hbm = f32[32,256,128]{2,1,0:T(8,128)} custom-call(f32[256,32,128]{2,1,0:T(8,128)} %b_hbm.5, s32[256,256]{1,0:T(8,128)S(1)} %copy-done, f32[32,128]{1,0:T(8,128)S(1)} %copy-done.1, f32[256,128]{1,0:T(8,128)S(1)} %get-tuple-element.19.cols_ref, f32[10,256,128]{2,1,0:T(8,128)S(1)} %get-tuple-element.20.tab_ref, ...), custom_call_target="tpu_custom_call" | custom-call | flops 12000000000 | bytes 24000000 | tf_op jit(solution)/shard_map/pallas_call | solution.py:470
  75.6 0.0 all-to-all-done.2.rx_ref
  75.6 4.1 %shard_map.79 = f32[256,32,128]{2,1,0:T(8,128)} custom-call(f32[32,256,128]{2,1,0:T(8,128)} %shard_map.78.o_hbm, f32[8,256,128]{2,1,0:T(8,128)S(1)} %all-to-all-done.2.rx_ref, f32[256,128]{1,0:T(8,128)S(1)} %get-tuple-element.19.cols_ref, f32[10,256,128]{2,1,0:T(8,128)S(1)} %get-tuple-element.20.tab_ref), custom_call_target="tpu_custom_call" | custom-call | flops 3000000000 | bytes 6000000 | tf_op jit(solution)/shard_map/pallas_call | solution.py:470
Async XLA Ops:
  0.0 10.8 %copy-start = (s32[256,256]{1,0:T(8,128)S(1)}, s32[256,256]{1,0:T(8,128)}, u32[]{:S(2)}) copy-start(s32[256,256]{1,0:T(8,128)} %adj_ref.3) | copy-start | bytes 786436
  0.0 10.8 %copy-start.1 = (f32[32,128]{1,0:T(8,128)S(1)}, f32[32,128]{1,0:T(8,128)}, u32[]{:S(2)}) copy-start(f32[32,128]{1,0:T(8,128)} %cap_ref.3) | copy-start | bytes 49156
  5.0 21.1 %all-to-all-start = ((f32[8,256,128]{2,1,0:T(8,128)}), f32[8,256,128]{2,1,0:T(8,128)S(1)}, u32[]{:S(2)}, u32[]{:S(2)}) async-start(f32[8,256,128]{2,1,0:T(8,128)} %get-tuple-element.23), calls=%async_computation | async-start | bytes 2097152 | tf_op jit(solution)/shard_map/all_to_all | solution.py:505
  27.8 26.5 %all-to-all-start.1 = ((f32[16,128,128]{2,1,0:T(8,128)}), f32[16,128,128]{2,1,0:T(8,128)S(1)}, u32[]{:S(2)}, u32[]{:S(2)}) async-start(f32[16,128,128]{2,1,0:T(8,128)} %get-tuple-element.28), calls=%async_computation.1 | async-start | bytes 2097152 | tf_op jit(solution)/shard_map/all_to_all | solution.py:517
  56.3 19.3 %all-to-all-start.2 = ((f32[8,256,128]{2,1,0:T(8,128)}), f32[8,256,128]{2,1,0:T(8,128)S(1)}, u32[]{:S(2)}, u32[]{:S(2)}) async-start(f32[8,256,128]{2,1,0:T(8,128)} %get-tuple-element.32), calls=%async_computation.2 | async-start | bytes 2097152 | tf_op jit(solution)/shard_map/all_to_all | solution.py:528

commit v3 on v2

--- a/solution.py
+++ b/solution.py
@@ -61,6 +61,12 @@
     return f * a + g * ia
 
 
+def smooth_and_total(v, a, ia, low, upp):
+    f = jnp.dot(split(v * ia), low, preferred_element_type=F32)
+    g = jnp.dot(split(v * a), upp, preferred_element_type=F32)
+    return f[:, :NYL] * a + g[:, :NYL] * ia, f[:, NYL:], g[:, NYL:]
+
+
 def respond(v, rcap, adj, adj_t, att, basal, level):
     p = jnp.maximum(v, 0.0)
     both = jnp.dot(adj_t, split(p), preferred_element_type=F32)
@@ -86,9 +92,14 @@
     return cf, cb
 
 
-def write_messages(msg_ref, front, back, me, count):
-    for k in range(count):
-        msg_ref[k] = jnp.where(k > me, front, back)
+def send_messages(sides, msg_hbm, sems, me, count):
+    copies = [
+        pltpu.make_async_copy(sides.at[(k > me).astype(jnp.int32)], msg_hbm.at[k], sems.at[k]) for k in range(count)
+    ]
+    for copy in copies:
+        copy.start()
+    for copy in copies:
+        copy.wait()
 
 
 def column_in(b_hbm, buf, sems, x):
@@ -116,7 +127,7 @@
     lax.fori_loop(first, last, body, 0)
 
 
-def tails_kernel(b_hbm, level_hbm, attack_hbm, rate_hbm, length_hbm, cols_ref, msg_ref, bt, level, vec, fr, ba, sems, vsems):
+def tails_kernel(b_hbm, level_hbm, attack_hbm, rate_hbm, length_hbm, cols_ref, msg_hbm, bt, level, vec, sides, sems, vsems, msems):
     sources = (length_hbm, rate_hbm, attack_hbm)
     small = [pltpu.make_async_copy(h, vec.at[pl.ds(k, 1), :], vsems.at[k]) for k, h in enumerate(sources)]
     small.append(pltpu.make_async_copy(level_hbm, level, vsems.at[3]))
@@ -141,17 +152,17 @@
             part = pl.ds(s0, CH)
             d = wide(cols_ref[part, DEC : DEC + 1])
             vs = [bt[x, part, :] for x in range(x0, x0 + BX)]
-            f = fr[part, :] if x0 else jnp.zeros((CH, NYL), F32)
+            f = sides[1, part, :] if x0 else jnp.zeros((CH, NYL), F32)
             for v in vs:
                 f = v + d * f
             g = vs[-1]
             for v in vs[-2::-1]:
                 g = v + d * g
             if x0:
-                g = ba[part, :] + wide(jnp.exp(-float(x0) * cols_ref[part, LAM : LAM + 1])) * g
-            fr[part, :] = f
-            ba[part, :] = g
-    write_messages(msg_ref, fr[...], ba[...], me, 8)
+                g = sides[0, part, :] + wide(jnp.exp(-float(x0) * cols_ref[part, LAM : LAM + 1])) * g
+            sides[1, part, :] = f
+            sides[0, part, :] = g
+    send_messages(sides, msg_hbm, msems, me, 8)
 
 
 def by_group(lane, parts):
@@ -189,13 +200,14 @@
 
 
 def first_kernel(
-    b_hbm, adj_ref, cap_ref, cols_ref, q_hbm, u_hbm, fun_ref, tab_ref, bt_ref, q_ref, u_ref, b_sems, q_sems, u_sems
+    b_hbm, adj_ref, cap_ref, cols_ref, q_hbm, fun_ref, tab_ref, bt_ref, q_ref, u_ref, f_ref, b_sems, q_sems
 ):
     each(0, NXL, lambda x: column_in(b_hbm, bt_ref, b_sems, x).start())
     cols = cols_ref[...]
     fill_tables(tab_ref, cols, lax.axis_index("gy"))
     web = food_web(adj_ref, cols)
-    rate = wide(col(cols, RATE))
+    rate, d = wide(col(cols, RATE)), wide(col(cols, DEC))
+    f_ref[...] = jnp.zeros_like(f_ref)
 
     def response(i, _):
         for j in range(BR):
@@ -206,53 +218,48 @@
             v = bt_ref[x]
             rcap = 1.0 / cap_ref[pl.ds(x, 1), :]
             q_ref[x] = v + time_step * (respond(v, rcap, *web) - rate * v)
-        for j in range(BR):
-            plane_out(q_ref, q_hbm, q_sems, i * BR + j).start()
+            f = v + d * f_ref[...]
+            f_ref[...] = f
+            u_ref[x] = f
         return 0
 
     lax.fori_loop(0, NXL // BR, response, 0)
 
-    def chunk(i, _):
-        part = pl.ds(pl.multiple_of(i * CH, CH), CH)
-        d = wide(cols_ref[part, DEC : DEC + 1])
-        wf, hf, wb, hb = (tab_ref[k, part, :] for k in (WF, FH, WB, BH))
-        lane = lanes(CH)
-
-        def fwd(k, f):
-            for j in range(BX):
-                x = k * BX + j
-                f = bt_ref[x, part, :] + d * f
-                u_ref[x, part, :] = f
-            return f
-
-        lax.fori_loop(0, NXL // BX, fwd, jnp.zeros((CH, NYL), F32))
-
-        def bwd(k, carry):
-            g, acc = carry
-            for j in range(BX):
-                x = NXL - 1 - (k * BX + j)
-                g = d * g
-                u = u_ref[x, part, :] + g
-                u_ref[x, part, :] = u
-                g = g + bt_ref[x, part, :]
-                q = q_ref[x, part, :]
-                acc = jnp.where(lane == x, lane_sum(wf * u), acc)
-                acc = jnp.where(lane == x + 32, lane_sum(wf * q + hf * u), acc)
-                acc = jnp.where(lane == x + 64, lane_sum(wb * u), acc)
-                acc = jnp.where(lane == x + 96, lane_sum(wb * q + hb * u), acc)
-            return g, acc
-
-        zero = jnp.zeros((CH, NYL), F32)
-        fun_ref[part, :] = lax.fori_loop(0, NXL // BX, bwd, (zero, zero))[1]
-        chunk_out(u_ref, u_hbm, u_sems, i).start()
+    low, upp = triangles()
+    ones = jnp.ones((2 * NYL, NYL), BF16)
+    low, upp = jnp.concatenate([low, ones], axis=1), jnp.concatenate([upp, ones], axis=1)
+    lam = col(cols, LAM)
+    c = wide(time_step * col(cols, RATE) * col(cols, NORM2))
+    lane = lanes(S)
+    y = lane.astype(F32) - 64.0
+    a, ia = jnp.exp(-lam * y), jnp.exp(lam * y)
+    f_ref[...] = jnp.zeros_like(f_ref)
+    fun_ref[...] = jnp.zeros_like(fun_ref)
+
+    def smoothing(i, _):
+        for j in range(BL):
+            x = NXL - 1 - (i * BL + j)
+            g = d * f_ref[...]
+            u = u_ref[x] + g
+            f_ref[...] = g + bt_ref[x]
+            smooth, total_f, total_b = smooth_and_total(u, a, ia, low, upp)
+            q = q_ref[x] + c * smooth
+            q_ref[x] = q
+            acc = jnp.where(lane == x, total_f, fun_ref[...])
+            acc = jnp.where(lane == x + 32, lane_sum(tab_ref[WF] * q), acc)
+            acc = jnp.where(lane == x + 64, total_b, acc)
+            fun_ref[...] = jnp.where(lane == x + 96, lane_sum(tab_ref[WB] * q), acc)
+        for j in range(BL):
+            plane_out(q_ref, q_hbm, q_sems, NXL - 1 - (i * BL + j)).start()
         return 0
 
-    lax.fori_loop(0, S // CH, chunk, 0)
+    lax.fori_loop(0, NXL // BL, smoothing, 0)
+    one = jnp.ones_like(lam)
+    fun_ref[...] = fun_ref[...] * by_group(lane, [jnp.exp(-63.0 * lam), one, jnp.exp(-64.0 * lam), one])
     each(0, NXL, lambda x: plane_out(q_ref, q_hbm, q_sems, x).wait())
-    each(0, S // CH, lambda i: chunk_out(u_ref, u_hbm, u_sems, i).wait())
-
-
-def rows_kernel(rx_ref, fun_ref, tab_ref, car_ref, own_ref, msg_ref):
+
+
+def rows_kernel(rx_ref, fun_ref, tab_ref, car_ref, own_ref, sides, msg_hbm, msems):
     mx, my = lax.axis_index("gx"), lax.axis_index("gy")
     cf, cb = read_carries(rx_ref, tab_ref[HOP_X], mx, 8)
     car_ref[0] = cf
@@ -265,19 +272,15 @@
     fun = fun + tab_ref[TURN] * tab_ref[HOP_Y] * pltpu.roll(fun, 96, 1)
     half = S // 2
     low_lanes = lanes(half) < 64
-    front = jnp.where(low_lanes, fun[:half], pltpu.roll(fun[half:], 64, 1))
-    back = jnp.where(low_lanes, pltpu.roll(fun[:half], 64, 1), fun[half:])
-    write_messages(msg_ref, front, back, my, 16)
+    sides[1] = jnp.where(low_lanes, fun[:half], pltpu.roll(fun[half:], 64, 1))
+    sides[0] = jnp.where(low_lanes, pltpu.roll(fun[:half], 64, 1), fun[half:])
+    send_messages(sides, msg_hbm, msems, my // 2, 8)
 
 
 def local_kernel(
-    u_hbm, q_hbm, car_ref, cols_ref, mid_hbm, p_hbm, tail_ref, u_ref, q_ref, up_ref, down_ref, u_sems, q_sems, p_sems, m_sems
+    q_hbm, car_ref, cols_ref, mid_hbm, p_hbm, tail_ref, q_ref, p_ref, up_ref, down_ref, q_sems, p_sems, m_sems
 ):
-    def fetch(x):
-        plane_in(u_hbm, u_ref, u_sems, x).start()
-        plane_in(q_hbm, q_ref, q_sems, x).start()
-
-    each(0, NXL, fetch)
+    each(0, NXL, lambda x: plane_in(q_hbm, q_ref, q_sems, x).start())
     cols = cols_ref[...]
     lam = col(cols, LAM)
     c = wide(time_step * col(cols, RATE) * col(cols, NORM2))
@@ -287,59 +290,83 @@
     a, ia = jnp.exp(-lam * y), jnp.exp(lam * y)
     low, upp = triangles()
     tail_ref[...] = jnp.zeros_like(tail_ref)
-    up_ref[...] = d
-    down_ref[...] = wide(jnp.exp(-32.0 * lam))
-
-    def step(i, _):
+    up_ref[...] = c * d * smooth_rows(car_ref[0], a, ia, low, upp)
+    down_ref[...] = c * jnp.exp(-32.0 * lam) * smooth_rows(car_ref[1], a, ia, low, upp)
+
+    def step(i, weight):
         for j in range(BL):
-            plane_in(u_hbm, u_ref, u_sems, i * BL + j).wait()
             plane_in(q_hbm, q_ref, q_sems, i * BL + j).wait()
         for j in range(BL):
             x = i * BL + j
             up, down = up_ref[...], down_ref[...]
-            u = u_ref[x] + up * car_ref[0] + down * car_ref[1]
-            mid = q_ref[x] + c * smooth_rows(u, a, ia, low, upp)
+            mid = q_ref[x] + up + down
             q_ref[x] = mid
             p = smooth_rows(mid, a, ia, low, upp)
-            u_ref[x] = p
+            p_ref[x] = p
             tail_ref[0] = p + d * tail_ref[0]
-            tail_ref[1] = tail_ref[1] + up * inv_d * p
+            tail_ref[1] = tail_ref[1] + weight * p
             up_ref[...] = up * d
             down_ref[...] = down * inv_d
+            weight = weight * col(cols, DEC)
         for j in range(BL):
             plane_out(q_ref, mid_hbm, m_sems, i * BL + j).start()
-            plane_out(u_ref, p_hbm, p_sems, i * BL + j).start()
-        return 0
-
-    lax.fori_loop(0, NXL // BL, step, 0)
+            plane_out(p_ref, p_hbm, p_sems, i * BL + j).start()
+        return weight
+
+    lax.fori_loop(0, NXL // BL, step, jnp.ones((S, 1), F32))
 
     def drain(x):
         plane_out(q_ref, mid_hbm, m_sems, x).wait()
-        plane_out(u_ref, p_hbm, p_sems, x).wait()
+        plane_out(p_ref, p_hbm, p_sems, x).wait()
 
     each(0, NXL, drain)
 
 
-def columns_kernel(ry_ref, own_ref, tail_ref, tab_ref, coef_ref, msg_ref):
-    mx, my = lax.axis_index("gx"), lax.axis_index("gy")
+def packed(low_lanes, v):
+    return jnp.where(low_lanes, v[: S // 2], v[S // 2 :])
+
+
+def chips_kernel(ry_ref, sides_ref, tab_ref, tail_ref, part_ref, msg_ref):
+    my = lax.axis_index("gy")
+    del tail_ref
+    chip, core = my // 2, my % 2
     half = S // 2
     low_lanes = lanes(half) < 64
-    hop = jnp.where(low_lanes, tab_ref[HOP_Y, :half, :], tab_ref[HOP_Y, half:, :])
+    hop = packed(low_lanes, tab_ref[HOP_Y])
+    run = packed(low_lanes, tab_ref[RUN])
+    hop2 = hop * hop
     zero = jnp.zeros((half, NYL), F32)
     lo, lo2, hi, hi2 = zero, zero, zero, zero
-    for k in range(15):
-        lo2 = jnp.where(k < my, hop * (lo2 + lo), lo2)
-        lo = jnp.where(k < my, ry_ref[k] + hop * lo, lo)
-    for k in range(15, 0, -1):
-        hi2 = jnp.where(k > my, hop * (hi2 + hi), hi2)
-        hi = jnp.where(k > my, ry_ref[k] + hop * hi, hi)
-
-    def unpack(low, high):
-        top = jnp.where(low_lanes, low, pltpu.roll(high, 64, 1))
-        bottom = jnp.where(low_lanes, pltpu.roll(low, 64, 1), high)
-        return jnp.concatenate([top, bottom], axis=0)
-
-    coef = unpack(lo, hi) + tab_ref[RUN] * pltpu.roll(unpack(lo2, hi2), 32, 1)
+    for k in range(7):
+        lo2 = jnp.where(k < chip, hop2 * (lo2 + lo), lo2)
+        lo = jnp.where(k < chip, ry_ref[k] + hop2 * lo, lo)
+    for k in range(7, 0, -1):
+        hi2 = jnp.where(k > chip, hop2 * (hi2 + hi), hi2)
+        hi = jnp.where(k > chip, ry_ref[k] + hop2 * hi, hi)
+
+    def same(z, z2):
+        return hop * z + run * pltpu.roll(hop * (2.0 * z2 + z), 32, 1)
+
+    def near(z, z2):
+        return z + run * pltpu.roll(2.0 * z2, 32, 1)
+
+    def far(z, z2):
+        return hop2 * z + run * pltpu.roll(2.0 * hop2 * (z2 + z), 32, 1)
+
+    part_ref[0] = same(lo, lo2)
+    part_ref[1] = same(hi, hi2)
+    msg_ref[0] = jnp.where(core == 0, far(lo, lo2) + sides_ref[1], near(lo, lo2))
+    msg_ref[1] = jnp.where(core == 1, far(hi, hi2) + sides_ref[0], near(hi, hi2))
+
+
+def columns_kernel(part_ref, other_ref, own_ref, tail_ref, tab_ref, coef_ref, msg_hbm, sides, msems):
+    mx = lax.axis_index("gx")
+    low_lanes = lanes(S // 2) < 64
+    lo = part_ref[0] + other_ref[0]
+    hi = part_ref[1] + other_ref[1]
+    top = jnp.where(low_lanes, lo, pltpu.roll(hi, 64, 1))
+    bottom = jnp.where(low_lanes, pltpu.roll(lo, 64, 1), hi)
+    coef = jnp.concatenate([top, bottom], axis=0)
     coef = coef + tab_ref[TURN] * pltpu.roll(own_ref[...] + tab_ref[HOP_Y] * coef, 96, 1)
     coef_ref[...] = coef
     lane = lanes(S)
@@ -350,12 +377,14 @@
         weight = tab_ref[table]
         front = front + lane_sum(jnp.where(inside, at_front, 0.0)) * weight
         back = back + lane_sum(jnp.where(inside, at_back, 0.0)) * weight
-    write_messages(msg_ref, front, back, mx, 8)
+    sides[1] = front
+    sides[0] = back
+    send_messages(sides, msg_hbm, msems, mx, 8)
 
 
 def second_kernel(
     b_hbm, adj_ref, cap_ref, cols_ref, tab_ref, mid_hbm, p_hbm, coef_ref, out_hbm,
-    out_ref, mid_ref, v_ref, roll_ref, b_sems, m_sems, p_sems, o_sems,
+    out_ref, mid_ref, v_ref, roll_ref, f_ref, b_sems, m_sems, p_sems, o_sems,
 ):
     def fetch(x):
         column_in(b_hbm, out_ref, b_sems, x).start()
@@ -368,7 +397,9 @@
     rate, d = wide(col(cols, RATE)), wide(col(cols, DEC))
     c = wide(time_step * col(cols, RATE) * col(cols, NORM2))
     ef, eb, alpha, beta = (d * tab_ref[k] for k in (WB, WF, BH, FH))
+    e = wide(0.5 * time_step * col(cols, RATE) * col(cols, NORM2))
     roll_ref[...] = coef_ref[...]
+    f_ref[...] = jnp.zeros_like(f_ref)
 
     def response(i, _):
         for j in range(BR):
@@ -382,10 +413,13 @@
             cfu, cfm, cbu, cbm = (coef[:, 32 * k : 32 * k + 1] for k in range(4))
             roll_ref[...] = pltpu.roll(coef, 127, 1)
             mid = mid_ref[x] + c * (cfu * ef + cbu * eb)
-            v_ref[x] = v_ref[x] + cfu * alpha + cbu * beta + cfm * ef + cbm * eb
+            v = v_ref[x] + cfu * alpha + cbu * beta + cfm * ef + cbm * eb
+            v_ref[x] = v
+            f = v + d * f_ref[...]
+            f_ref[...] = f
             rcap = 1.0 / cap_ref[pl.ds(x, 1), :]
             r = respond(mid, rcap, *web)
-            out_ref[x] = 0.5 * (out_ref[x] + mid) + 0.5 * time_step * (r - rate * mid)
+            out_ref[x] = 0.5 * (out_ref[x] + mid) + 0.5 * time_step * (r - rate * mid) + e * f
         return 0
 
     lax.fori_loop(0, NXL // BR, response, 0)
@@ -394,15 +428,6 @@
         part = pl.ds(pl.multiple_of(i * CH, CH), CH)
         d = wide(cols_ref[part, DEC : DEC + 1])
         e = wide(0.5 * time_step * cols_ref[part, RATE : RATE + 1] * cols_ref[part, NORM2 : NORM2 + 1])
-
-        def fwd(k, f):
-            for j in range(BX):
-                x = k * BX + j
-                f = v_ref[x, part, :] + d * f
-                out_ref[x, part, :] = out_ref[x, part, :] + e * f
-            return f
-
-        lax.fori_loop(0, NXL // BX, fwd, jnp.zeros((CH, NYL), F32))
 
         def bwd(k, g):
             for j in range(BX):
@@ -483,10 +508,15 @@
     plane = pltpu.VMEM(PLANE, F32)
     columns = pltpu.SemaphoreType.DMA((NXL,))
     chunks = pltpu.SemaphoreType.DMA((S // CH,))
+    x_sides = [pltpu.VMEM((2,) + PLANE, F32), pltpu.SemaphoreType.DMA((8,))]
+    same_core = [[core + 2 * chip for chip in range(8)] for core in range(2)]
+    other_core = [(k, k ^ 1) for k in range(16)]
     field_out = (pltpu.HBM(FIELD, F32), HBM)
     plane_out = (plane, VM)
-    x_out = (pltpu.HBM((8,) + PLANE, F32), VM)
-    y_out = (pltpu.HBM((16, S // 2, NYL), F32), VM)
+    x_out = (pltpu.HBM((8,) + PLANE, F32), HBM)
+    y_out = (pltpu.HBM((8, S // 2, NYL), F32), HBM)
+    halves_out = (pltpu.VMEM((2, S // 2, NYL), F32), VM)
+    to_core = (jax.ShapeDtypeStruct((2, S // 2, NYL), F32), VM)
     pair_out = (pltpu.VMEM((2,) + PLANE, F32), VM)
     tables_out = (pltpu.VMEM((10,) + PLANE, F32), VM)
     result = (pltpu.HBM((S, NXL, NYL), F32), HBM)
@@ -498,39 +528,45 @@
         tails_kernel,
         [b] + vectors,
         [plane_out, x_out],
-        [field, pltpu.VMEM((1, S), jnp.int32), pltpu.VMEM((8, S), F32), plane, plane, columns, pltpu.SemaphoreType.DMA((4,))],
+        [field, pltpu.VMEM((1, S), jnp.int32), pltpu.VMEM((8, S), F32), x_sides[0], columns, pltpu.SemaphoreType.DMA((4,)), x_sides[1]],
         3,
     )
     cols = (in_vmem(cols), VM)
     rx = in_vmem(lax.all_to_all(msg, "gx", 0, 0))
-    q, u, fun, tab = call(
+    q, fun, tab = call(
         first_kernel,
         [b, adj, cap, cols],
-        [field_out, field_out, plane_out, tables_out],
-        [field, field, field, columns, columns, chunks],
+        [field_out, plane_out, tables_out],
+        [field, field, field, plane, columns, columns],
         12,
     )
     tab = (in_vmem(tab), VM)
-    car, own, msg = call(
-        rows_kernel, [(rx, VM), (in_vmem(fun), VM), tab], [pair_out, plane_out, y_out], [], 1
-    )
-    ry = in_vmem(lax.all_to_all(msg, "gy", 0, 0))
+    car, own, sides, msg = call(
+        rows_kernel,
+        [(rx, VM), (in_vmem(fun), VM), tab],
+        [pair_out, plane_out, halves_out, y_out],
+        [pltpu.SemaphoreType.DMA((8,))],
+        1,
+    )
+    ry = in_vmem(lax.all_to_all(msg, "gy", 0, 0, axis_index_groups=same_core))
     mid, p, tail = call(
         local_kernel,
-        [(u, HBM), (q, HBM), (in_vmem(car), VM), cols],
+        [(q, HBM), (in_vmem(car), VM), cols],
         [field_out, field_out, pair_out],
-        [field, field, plane, plane, columns, columns, columns, columns],
+        [field, field, plane, plane, columns, columns, columns],
         12,
     )
+    part, msg = call(chips_kernel, [(ry, VM), (in_vmem(sides), VM), tab, (in_vmem(tail), VM)], [halves_out, to_core], [], 1)
+    other = lax.ppermute(msg, "gy", other_core)
     coef, msg = call(
-        columns_kernel, [(ry, VM), (in_vmem(own), VM), (in_vmem(tail), VM), tab], [plane_out, x_out], [], 1
+        columns_kernel, [(in_vmem(part), VM), (other, VM), (in_vmem(own), VM), (in_vmem(tail), VM), tab], [plane_out, x_out], x_sides, 1
     )
     rx = in_vmem(lax.all_to_all(msg, "gx", 0, 0))
     (part,) = call(
         second_kernel,
         [b, adj, cap, cols, tab, (mid, HBM), (p, HBM), (in_vmem(coef), VM)],
         [field_out],
-        [field, field, field, plane, columns, columns, columns, chunks],
+        [field, field, field, plane, plane, columns, columns, columns, chunks],
         12,
     )
     (out,) = call(

time: 80.1 us -> 74.4 us (0.929)
  Pallas kernels: 54.9 us -> 48.3 us
  starting transfers between devices: 18.7 us -> 20.3 us
    pallas_call x7 -> x8, Pallas kernels: 54.9 us -> 48.3 us  [call(): pl.pallas_call(kernel, out_shape=[shape for shape, _ in outs], in_specs=[...]
    all_to_all x1, waiting for transfers between devices: 5.19 us -> 1.49 us  [shards(): ry = in_vmem(lax.all_to_all(msg, 'gy', 0, 0, axis_index_groups=same_core))]
    ppermute x0 -> x1, starting transfers between devices: none -> 3.44 us  [shards(): other = lax.ppermute(msg, 'gy', other_core)]
    all_to_all x2, waiting for transfers between devices: 0.91 us -> 2.98 us  [shards(): rx = in_vmem(lax.all_to_all(msg, 'gx', 0, 0))]
    all_to_all x1, starting transfers between devices: 9.29 us -> 7.38 us  [shards(): ry = in_vmem(lax.all_to_all(msg, 'gy', 0, 0, axis_index_groups=same_core))]
    ppermute x0 -> x1, waiting for transfers between devices: none -> 0.99 us  [shards(): other = lax.ppermute(msg, 'gy', other_core)]
  transfers between devices with their start and end apart: 3 -> 4, of which waited for: 2 -> 4; matrix products, arithmetic and copies ran while one was open for 0% -> 0% of each run, Pallas kernels for 53% -> 48%
where the time goes in v3:
time: 74.4 us; the launch traced here: 74.1 us
  Pallas kernels  48.3 us (65%)
  starting transfers between devices  20.3 us (27%)
  waiting for transfers between devices  5.45 us (7%)
    pallas_call x8, Pallas kernels, call(): pl.pallas_call(kernel, out_shape=[shape for shape, _ in outs], in_specs=[...  48.3 us
    all_to_all x2, starting transfers between devices, shards(): rx = in_vmem(lax.all_to_all(msg, 'gx', 0, 0))  9.45 us
    all_to_all x1, starting transfers between devices, shards(): ry = in_vmem(lax.all_to_all(msg, 'gy', 0, 0, axis_index_groups=same_core))  7.38 us
    ppermute x1, starting transfers between devices, shards(): other = lax.ppermute(msg, 'gy', other_core)  3.44 us
    all_to_all x2, waiting for transfers between devices, shards(): rx = in_vmem(lax.all_to_all(msg, 'gx', 0, 0))  2.98 us
    all_to_all x1, waiting for transfers between devices, shards(): ry = in_vmem(lax.all_to_all(msg, 'gy', 0, 0, axis_index_groups=same_core))  1.49 us
  transfers between devices with their start and end apart: 4, of which 4 were waited for; matrix products, arithmetic and copies ran while one was open for 0% of the time, Pallas kernels for 48%

profile of v3, /device:TPU:1, one launch (start us, length us, event | category | flops | bytes accessed | tf_op | source)
XLA Modules:
  0.0 74.1 jit_solution(3099509544747087294)
XLA Ops:
  0.0 0.0 copy-start
  0.0 0.0 copy-start.1
  0.0 5.0 %shard_map.73 = (f32[256,128]{1,0:T(8,128)S(1)}, f32[8,256,128]{2,1,0:T(8,128)}) custom-call(f32[256,32,128]{2,1,0:T(8,128)} %b_hbm.5, s32[1,256]{1,0:T(1,128)} %bitcast.4, f32[1,256]{1,0:T(1,128)} %bitcast.5, f32[1,256]{1,0:T(1,128)} %bitcast.6, f32[1,256]{1,0:T(1,128)} %bitcast.7), custom_call_target="tpu_custom_call" | custom-call | flops 3000000000 | bytes 6000000 | tf_op jit(solution)/shard_map/pallas_call | solution.py:495
  5.0 5.9 %all-to-all-start = ((f32[8,256,128]{2,1,0:T(8,128)}), f32[8,256,128]{2,1,0:T(8,128)S(1)}, u32[]{:S(2)}, u32[]{:S(2)}) async-start(f32[8,256,128]{2,1,0:T(8,128)} %get-tuple-element.24), calls=%async_computation | async-start | bytes 2097152 | tf_op jit(solution)/shard_map/all_to_all | solution.py:535
  10.9 0.0 copy-done
  10.9 0.0 copy-done.1
  10.9 12.9 %shard_map.74 = (f32[32,256,128]{2,1,0:T(8,128)}, f32[256,128]{1,0:T(8,128)S(1)}, f32[10,256,128]{2,1,0:T(8,128)S(1)}) custom-call(f32[256,32,128]{2,1,0:T(8,128)} %b_hbm.5, s32[256,256]{1,0:T(8,128)S(1)} %copy-done, f32[32,128]{1,0:T(8,128)S(1)} %copy-done.1, f32[256,128]{1,0:T(8,128)S(1)} %get-tuple-element.21.cols_ref), custom_call_target="tpu_custom_call" | custom-call | flops 12000000000 | bytes 24000000 | tf_op jit(solution)/shard_map/pallas_call | solution.py:495
  23.7 2.3 %all-to-all-done.rx_ref = f32[8,256,128]{2,1,0:T(8,128)S(1)} async-done(((f32[8,256,128]{2,1,0:T(8,128)}), f32[8,256,128]{2,1,0:T(8,128)S(1)}, u32[]{:S(2)}, u32[]{:S(2)}) %all-to-all-start) | async-done | bytes 1048608 | tf_op jit(solution)/shard_map/all_to_all | solution.py:535
  26.0 1.6 %shard_map.75 = (f32[2,256,128]{2,1,0:T(8,128)S(1)}, f32[256,128]{1,0:T(8,128)S(1)}, f32[2,128,128]{2,1,0:T(8,128)S(1)}, f32[8,128,128]{2,1,0:T(8,128)}) custom-call(f32[8,256,128]{2,1,0:T(8,128)S(1)} %all-to-all-done.rx_ref, f32[256,128]{1,0:T(8,128)S(1)} %get-tuple-element.25.fun_ref, f32[10,256,128]{2,1,0:T(8,128)S(1)} %get-tuple-element.22.tab_ref), custom_call_target="tpu_custom_call" | custom-call | flops 1000000000 | bytes 2000000 | tf_op jit(solution)/shard_map/pallas_call | solution.py:495
  27.6 7.4 %all-to-all-start.1 = ((f32[8,128,128]{2,1,0:T(8,128)}), f32[8,128,128]{2,1,0:T(8,128)S(1)}, u32[]{:S(2)}, u32[]{:S(2)}) async-start(f32[8,128,128]{2,1,0:T(8,128)} %get-tuple-element.29), calls=%async_computation.1 | async-start | bytes 1048576 | tf_op jit(solution)/shard_map/all_to_all | solution.py:551
  35.0 7.3 %shard_map.76 = (f32[32,256,128]{2,1,0:T(8,128)}, f32[32,256,128]{2,1,0:T(8,128)}, f32[2,256,128]{2,1,0:T(8,128)S(1)}) custom-call(f32[32,256,128]{2,1,0:T(8,128)} %get-tuple-element.23.q_hbm, f32[2,256,128]{2,1,0:T(8,128)S(1)} %get-tuple-element.26.car_ref, f32[256,128]{1,0:T(8,128)S(1)} %get-tuple-element.21.cols_ref), custom_call_target="tpu_custom_call" | custom-call | flops 12000000000 | bytes 24000000 | tf_op jit(solution)/shard_map/pallas_call | solution.py:495
  42.3 1.5 %all-to-all-done.1.ry_ref = f32[8,128,128]{2,1,0:T(8,128)S(1)} async-done(((f32[8,128,128]{2,1,0:T(8,128)}), f32[8,128,128]{2,1,0:T(8,128)S(1)}, u32[]{:S(2)}, u32[]{:S(2)}) %all-to-all-start.1) | async-done | bytes 524320 | tf_op jit(solution)/shard_map/all_to_all | solution.py:551
  43.8 0.3 shard_map.77
  44.1 3.4 %collective-permute-start = (f32[2,128,128]{2,1,0:T(8,128)S(1)}, f32[2,128,128]{2,1,0:T(8,128)S(1)}, u32[]{:S(2)}, u32[]{:S(2)}) collective-permute-start(f32[2,128,128]{2,1,0:T(8,128)S(1)} %get-tuple-element.33), channel_id=1, source_target_pairs={{0,1},{1,0},{2,3},{3,2},{4,5},{5,4},{6,7},{7,6},{8,9},{9,8},{10,11... | collective-permute-start | bytes 393224 | tf_op jit(solution)/shard_map/ppermute | solution.py:560
  47.6 1.0 %collective-permute-done.other_ref = f32[2,128,128]{2,1,0:T(8,128)S(1)} collective-permute-done((f32[2,128,128]{2,1,0:T(8,128)S(1)}, f32[2,128,128]{2,1,0:T(8,128)S(1)}, u32[]{:S(2)}, u32[]{:S(2)}) %collective-permute-start) | collective-permute-done | bytes 131104 | tf_op jit(solution)/shard_map/ppermute | solution.py:560
  48.6 1.5 %shard_map.78 = (f32[256,128]{1,0:T(8,128)S(1)}, f32[8,256,128]{2,1,0:T(8,128)}) custom-call(f32[2,128,128]{2,1,0:T(8,128)S(1)} %get-tuple-element.32.part_ref, f32[2,128,128]{2,1,0:T(8,128)S(1)} %collective-permute-done.other_ref, f32[256,128]{1,0:T(8,128)S(1)} %get-tuple-element.34.own_ref, f32[2,256,128]{2,1,0:T(8,128)S(1)} %get-tuple-element.31.tail_ref, ...), custom_call_target="tpu_custom_call" | custom-call | flops 1000000000 | bytes 2000000 | tf_op jit(solution)/shard_map/pallas_call | solution.py:495
  50.1 3.6 %all-to-all-start.2 = ((f32[8,256,128]{2,1,0:T(8,128)}), f32[8,256,128]{2,1,0:T(8,128)S(1)}, u32[]{:S(2)}, u32[]{:S(2)}) async-start(f32[8,256,128]{2,1,0:T(8,128)} %get-tuple-element.36), calls=%async_computation.2 | async-start | bytes 2097152 | tf_op jit(solution)/shard_map/all_to_all | solution.py:564
  53.7 15.6 %shard_map.79.o_hbm = f32[32,256,128]{2,1,0:T(8,128)} custom-call(f32[256,32,128]{2,1,0:T(8,128)} %b_hbm.5, s32[256,256]{1,0:T(8,128)S(1)} %copy-done, f32[32,128]{1,0:T(8,128)S(1)} %copy-done.1, f32[256,128]{1,0:T(8,128)S(1)} %get-tuple-element.21.cols_ref, f32[10,256,128]{2,1,0:T(8,128)S(1)} %get-tuple-element.22.tab_ref, ...), custom_call_target="tpu_custom_call" | custom-call | flops 12000000000 | bytes 24000000 | tf_op jit(solution)/shard_map/pallas_call | solution.py:495
  69.3 0.7 all-to-all-done.2.rx_ref
  70.0 4.1 %shard_map.80 = f32[256,32,128]{2,1,0:T(8,128)} custom-call(f32[32,256,128]{2,1,0:T(8,128)} %shard_map.79.o_hbm, f32[8,256,128]{2,1,0:T(8,128)S(1)} %all-to-all-done.2.rx_ref, f32[256,128]{1,0:T(8,128)S(1)} %get-tuple-element.21.cols_ref, f32[10,256,128]{2,1,0:T(8,128)S(1)} %get-tuple-element.22.tab_ref), custom_call_target="tpu_custom_call" | custom-call | flops 3000000000 | bytes 6000000 | tf_op jit(solution)/shard_map/pallas_call | solution.py:495
Async XLA Ops:
  0.0 10.9 %copy-start = (s32[256,256]{1,0:T(8,128)S(1)}, s32[256,256]{1,0:T(8,128)}, u32[]{:S(2)}) copy-start(s32[256,256]{1,0:T(8,128)} %adj_ref.3) | copy-start | bytes 786436
  0.0 10.9 %copy-start.1 = (f32[32,128]{1,0:T(8,128)S(1)}, f32[32,128]{1,0:T(8,128)}, u32[]{:S(2)}) copy-start(f32[32,128]{1,0:T(8,128)} %cap_ref.3) | copy-start | bytes 49156
  5.0 21.1 %all-to-all-start = ((f32[8,256,128]{2,1,0:T(8,128)}), f32[8,256,128]{2,1,0:T(8,128)S(1)}, u32[]{:S(2)}, u32[]{:S(2)}) async-start(f32[8,256,128]{2,1,0:T(8,128)} %get-tuple-element.24), calls=%async_computation | async-start | bytes 2097152 | tf_op jit(solution)/shard_map/all_to_all | solution.py:535
  27.6 16.2 %all-to-all-start.1 = ((f32[8,128,128]{2,1,0:T(8,128)}), f32[8,128,128]{2,1,0:T(8,128)S(1)}, u32[]{:S(2)}, u32[]{:S(2)}) async-start(f32[8,128,128]{2,1,0:T(8,128)} %get-tuple-element.29), calls=%async_computation.1 | async-start | bytes 1048576 | tf_op jit(solution)/shard_map/all_to_all | solution.py:551
  44.1 4.4 %collective-permute-start = (f32[2,128,128]{2,1,0:T(8,128)S(1)}, f32[2,128,128]{2,1,0:T(8,128)S(1)}, u32[]{:S(2)}, u32[]{:S(2)}) collective-permute-start(f32[2,128,128]{2,1,0:T(8,128)S(1)} %get-tuple-element.33), channel_id=1, source_target_pairs={{0,1},{1,0},{2,3},{3,2},{4,5},{5,4},{6,7},{7,6},{8,9},{9,8},{10,11... | collective-permute-start | bytes 393224 | tf_op jit(solution)/shard_map/ppermute | solution.py:560
  50.1 19.9 %all-to-all-start.2 = ((f32[8,256,128]{2,1,0:T(8,128)}), f32[8,256,128]{2,1,0:T(8,128)S(1)}, u32[]{:S(2)}, u32[]{:S(2)}) async-start(f32[8,256,128]{2,1,0:T(8,128)} %get-tuple-element.36), calls=%async_computation.2 | async-start | bytes 2097152 | tf_op jit(solution)/shard_map/all_to_all | solution.py:564

commit v4 on v3

--- a/solution.py
+++ b/solution.py
@@ -17,6 +17,7 @@
 BX = 8
 BR = 4
 BL = 4
+TURN_BY = 2
 F32 = jnp.float32
 BF16 = jnp.bfloat16
 VMEM_LIMIT = 32 * 1024 * 1024
@@ -82,19 +83,23 @@
     return (adj.astype(BF16), adj.T.astype(BF16)) + tuple(wide(col(cols, k)) for k in (ATT, BASAL, LEVEL))
 
 
-def read_carries(rx_ref, hop, me, count):
+def read_carries(rx_ref, hop, me, count, slot):
     cf = jnp.zeros(rx_ref.shape[1:], F32)
     cb = jnp.zeros(rx_ref.shape[1:], F32)
     for k in range(count):
-        cf = jnp.where(k < me, rx_ref[k] + hop * cf, cf)
+        cf = jnp.where(k < me, rx_ref[slot(k)] + hop * cf, cf)
     for k in range(count - 1, -1, -1):
-        cb = jnp.where(k > me, rx_ref[k] + hop * cb, cb)
+        cb = jnp.where(k > me, rx_ref[slot(k)] + hop * cb, cb)
     return cf, cb
 
 
-def send_messages(sides, msg_hbm, sems, me, count):
+def column_slot(k):
+    return (k + 8 - TURN_BY * (lax.axis_index("gy") % 2)) % 8
+
+
+def send_messages(sides, msg_hbm, sems, me, count, slot):
     copies = [
-        pltpu.make_async_copy(sides.at[(k > me).astype(jnp.int32)], msg_hbm.at[k], sems.at[k]) for k in range(count)
+        pltpu.make_async_copy(sides.at[(k > me).astype(jnp.int32)], msg_hbm.at[slot(k)], sems.at[k]) for k in range(count)
     ]
     for copy in copies:
         copy.start()
@@ -162,7 +167,7 @@
                 g = sides[0, part, :] + wide(jnp.exp(-float(x0) * cols_ref[part, LAM : LAM + 1])) * g
             sides[1, part, :] = f
             sides[0, part, :] = g
-    send_messages(sides, msg_hbm, msems, me, 8)
+    send_messages(sides, msg_hbm, msems, me, 8, column_slot)
 
 
 def by_group(lane, parts):
@@ -261,7 +266,7 @@
 
 def rows_kernel(rx_ref, fun_ref, tab_ref, car_ref, own_ref, sides, msg_hbm, msems):
     mx, my = lax.axis_index("gx"), lax.axis_index("gy")
-    cf, cb = read_carries(rx_ref, tab_ref[HOP_X], mx, 8)
+    cf, cb = read_carries(rx_ref, tab_ref[HOP_X], mx, 8, column_slot)
     car_ref[0] = cf
     car_ref[1] = cb
     lane = lanes(S)
@@ -274,7 +279,7 @@
     low_lanes = lanes(half) < 64
     sides[1] = jnp.where(low_lanes, fun[:half], pltpu.roll(fun[half:], 64, 1))
     sides[0] = jnp.where(low_lanes, pltpu.roll(fun[:half], 64, 1), fun[half:])
-    send_messages(sides, msg_hbm, msems, my // 2, 8)
+    send_messages(sides, msg_hbm, msems, my // 2, 8, lambda k: k)
 
 
 def local_kernel(
@@ -379,7 +384,7 @@
         back = back + lane_sum(jnp.where(inside, at_back, 0.0)) * weight
     sides[1] = front
     sides[0] = back
-    send_messages(sides, msg_hbm, msems, mx, 8)
+    send_messages(sides, msg_hbm, msems, mx, 8, column_slot)
 
 
 def second_kernel(
@@ -452,7 +457,7 @@
     cols = cols_ref[...]
     lam = col(cols, LAM)
     e = 0.5 * time_step * col(cols, RATE) * col(cols, NORM2)
-    cf, cb = read_carries(rx_ref, tab_ref[HOP_X], lax.axis_index("gx"), 8)
+    cf, cb = read_carries(rx_ref, tab_ref[HOP_X], lax.axis_index("gx"), 8, column_slot)
     cf_ref[...] = cf * (e * col(cols, DEC))
     cb_ref[...] = cb * (e * jnp.exp(-32.0 * lam))
     copies = [pltpu.make_async_copy(buf.at[x], out_hbm.at[:, x, :], sems.at[x]) for x in range(NXL)]
@@ -509,6 +514,7 @@
     columns = pltpu.SemaphoreType.DMA((NXL,))
     chunks = pltpu.SemaphoreType.DMA((S // CH,))
     x_sides = [pltpu.VMEM((2,) + PLANE, F32), pltpu.SemaphoreType.DMA((8,))]
+    same_row = [[(k + TURN_BY * (row % 2)) % 8 * 16 + row for k in range(8)] for row in range(16)]
     same_core = [[core + 2 * chip for chip in range(8)] for core in range(2)]
     other_core = [(k, k ^ 1) for k in range(16)]
     field_out = (pltpu.HBM(FIELD, F32), HBM)
@@ -532,7 +538,7 @@
         3,
     )
     cols = (in_vmem(cols), VM)
-    rx = in_vmem(lax.all_to_all(msg, "gx", 0, 0))
+    rx = in_vmem(lax.all_to_all(msg, ("gx", "gy"), 0, 0, axis_index_groups=same_row))
     q, fun, tab = call(
         first_kernel,
         [b, adj, cap, cols],
@@ -561,7 +567,7 @@
     coef, msg = call(
         columns_kernel, [(in_vmem(part), VM), (other, VM), (in_vmem(own), VM), (in_vmem(tail), VM), tab], [plane_out, x_out], x_sides, 1
     )
-    rx = in_vmem(lax.all_to_all(msg, "gx", 0, 0))
+    rx = in_vmem(lax.all_to_all(msg, ("gx", "gy"), 0, 0, axis_index_groups=same_row))
     (part,) = call(
         second_kernel,
         [b, adj, cap, cols, tab, (mid, HBM), (p, HBM), (in_vmem(coef), VM)],

time: 74.4 us -> 73.2 us (0.984)
  waiting for transfers between devices: 5.45 us -> 2.98 us
  starting transfers between devices: 20.3 us -> 21.4 us
    all_to_all x2, waiting for transfers between devices: 2.98 us -> 0.44 us  [shards(): lax.all_to_all(msg, ('gx', 'gy'), 0, 0, axis_index_groups=same_row)]
    all_to_all x2, starting transfers between devices: 9.45 us -> 10.5 us  [shards(): lax.all_to_all(msg, ('gx', 'gy'), 0, 0, axis_index_groups=same_row)]
  transfers between devices with their start and end apart: 4 -> 4, of which waited for: 4 -> 3; matrix products, arithmetic and copies ran while one was open for 0% -> 0% of each run, Pallas kernels for 48% -> 49%
where the time goes in v4:
time: 73.2 us; the launch traced here: 72.9 us
  Pallas kernels  48.4 us (66%)
  starting transfers between devices  21.4 us (29%)
  waiting for transfers between devices  2.98 us (4%)
    pallas_call x8, Pallas kernels, call(): pl.pallas_call(kernel, out_shape=[shape for shape, _ in outs], in_specs=[...  48.4 us
    all_to_all x2, starting transfers between devices, shards(): lax.all_to_all(msg, ('gx', 'gy'), 0, 0, axis_index_groups=same_row)  10.5 us
    all_to_all x1, starting transfers between devices, shards(): ry = in_vmem(lax.all_to_all(msg, 'gy', 0, 0, axis_index_groups=same_core))  7.38 us
    ppermute x1, starting transfers between devices, shards(): other = lax.ppermute(msg, 'gy', other_core)  3.45 us
    all_to_all x1, waiting for transfers between devices, shards(): ry = in_vmem(lax.all_to_all(msg, 'gy', 0, 0, axis_index_groups=same_core))  1.55 us
  transfers between devices with their start and end apart: 4, of which 3 were waited for; matrix products, arithmetic and copies ran while one was open for 0% of the time, Pallas kernels for 49%

profile of v4, /device:TPU:1, one launch (start us, length us, event | category | flops | bytes accessed | tf_op | source)
XLA Modules:
  0.0 72.9 jit_solution(14596365684622864365)
XLA Ops:
  0.0 0.0 copy-start
  0.0 0.0 copy-start.1
  0.0 5.0 %shard_map.73 = (f32[256,128]{1,0:T(8,128)S(1)}, f32[8,256,128]{2,1,0:T(8,128)}) custom-call(f32[256,32,128]{2,1,0:T(8,128)} %b_hbm.5, s32[1,256]{1,0:T(1,128)} %bitcast.4, f32[1,256]{1,0:T(1,128)} %bitcast.5, f32[1,256]{1,0:T(1,128)} %bitcast.6, f32[1,256]{1,0:T(1,128)} %bitcast.7), custom_call_target="tpu_custom_call" | custom-call | flops 3000000000 | bytes 6000000 | tf_op jit(solution)/shard_map/pallas_call | solution.py:500
  5.0 6.2 %all-to-all-start = ((f32[8,256,128]{2,1,0:T(8,128)}), f32[8,256,128]{2,1,0:T(8,128)S(1)}, u32[]{:S(2)}, u32[]{:S(2)}) async-start(f32[8,256,128]{2,1,0:T(8,128)} %get-tuple-element.24), calls=%async_computation | async-start | bytes 2097152 | tf_op jit(solution)/shard_map/all_to_all | solution.py:541
  11.2 0.0 copy-done
  11.2 0.0 copy-done.1
  11.2 12.9 %shard_map.74 = (f32[32,256,128]{2,1,0:T(8,128)}, f32[256,128]{1,0:T(8,128)S(1)}, f32[10,256,128]{2,1,0:T(8,128)S(1)}) custom-call(f32[256,32,128]{2,1,0:T(8,128)} %b_hbm.5, s32[256,256]{1,0:T(8,128)S(1)} %copy-done, f32[32,128]{1,0:T(8,128)S(1)} %copy-done.1, f32[256,128]{1,0:T(8,128)S(1)} %get-tuple-element.21.cols_ref), custom_call_target="tpu_custom_call" | custom-call | flops 12000000000 | bytes 24000000 | tf_op jit(solution)/shard_map/pallas_call | solution.py:500
  24.1 0.4 all-to-all-done.rx_ref
  24.5 1.6 %shard_map.75 = (f32[2,256,128]{2,1,0:T(8,128)S(1)}, f32[256,128]{1,0:T(8,128)S(1)}, f32[2,128,128]{2,1,0:T(8,128)S(1)}, f32[8,128,128]{2,1,0:T(8,128)}) custom-call(f32[8,256,128]{2,1,0:T(8,128)S(1)} %all-to-all-done.rx_ref, f32[256,128]{1,0:T(8,128)S(1)} %get-tuple-element.25.fun_ref, f32[10,256,128]{2,1,0:T(8,128)S(1)} %get-tuple-element.22.tab_ref), custom_call_target="tpu_custom_call" | custom-call | flops 1000000000 | bytes 2000000 | tf_op jit(solution)/shard_map/pallas_call | solution.py:500
  26.1 7.4 %all-to-all-start.1 = ((f32[8,128,128]{2,1,0:T(8,128)}), f32[8,128,128]{2,1,0:T(8,128)S(1)}, u32[]{:S(2)}, u32[]{:S(2)}) async-start(f32[8,128,128]{2,1,0:T(8,128)} %get-tuple-element.29), calls=%async_computation.1 | async-start | bytes 1048576 | tf_op jit(solution)/shard_map/all_to_all | solution.py:557
  33.5 7.3 %shard_map.76 = (f32[32,256,128]{2,1,0:T(8,128)}, f32[32,256,128]{2,1,0:T(8,128)}, f32[2,256,128]{2,1,0:T(8,128)S(1)}) custom-call(f32[32,256,128]{2,1,0:T(8,128)} %get-tuple-element.23.q_hbm, f32[2,256,128]{2,1,0:T(8,128)S(1)} %get-tuple-element.26.car_ref, f32[256,128]{1,0:T(8,128)S(1)} %get-tuple-element.21.cols_ref), custom_call_target="tpu_custom_call" | custom-call | flops 12000000000 | bytes 24000000 | tf_op jit(solution)/shard_map/pallas_call | solution.py:500
  40.8 1.6 %all-to-all-done.1.ry_ref = f32[8,128,128]{2,1,0:T(8,128)S(1)} async-done(((f32[8,128,128]{2,1,0:T(8,128)}), f32[8,128,128]{2,1,0:T(8,128)S(1)}, u32[]{:S(2)}, u32[]{:S(2)}) %all-to-all-start.1) | async-done | bytes 524320 | tf_op jit(solution)/shard_map/all_to_all | solution.py:557
  42.3 0.3 shard_map.77
  42.7 3.4 %collective-permute-start = (f32[2,128,128]{2,1,0:T(8,128)S(1)}, f32[2,128,128]{2,1,0:T(8,128)S(1)}, u32[]{:S(2)}, u32[]{:S(2)}) collective-permute-start(f32[2,128,128]{2,1,0:T(8,128)S(1)} %get-tuple-element.33), channel_id=1, source_target_pairs={{0,1},{1,0},{2,3},{3,2},{4,5},{5,4},{6,7},{7,6},{8,9},{9,8},{10,11... | collective-permute-start | bytes 393224 | tf_op jit(solution)/shard_map/ppermute | solution.py:566
  46.1 1.0 %collective-permute-done.other_ref = f32[2,128,128]{2,1,0:T(8,128)S(1)} collective-permute-done((f32[2,128,128]{2,1,0:T(8,128)S(1)}, f32[2,128,128]{2,1,0:T(8,128)S(1)}, u32[]{:S(2)}, u32[]{:S(2)}) %collective-permute-start) | collective-permute-done | bytes 131104 | tf_op jit(solution)/shard_map/ppermute | solution.py:566
  47.1 1.5 %shard_map.78 = (f32[256,128]{1,0:T(8,128)S(1)}, f32[8,256,128]{2,1,0:T(8,128)}) custom-call(f32[2,128,128]{2,1,0:T(8,128)S(1)} %get-tuple-element.32.part_ref, f32[2,128,128]{2,1,0:T(8,128)S(1)} %collective-permute-done.other_ref, f32[256,128]{1,0:T(8,128)S(1)} %get-tuple-element.34.own_ref, f32[2,256,128]{2,1,0:T(8,128)S(1)} %get-tuple-element.31.tail_ref, ...), custom_call_target="tpu_custom_call" | custom-call | flops 1000000000 | bytes 2000000 | tf_op jit(solution)/shard_map/pallas_call | solution.py:500
  48.6 4.3 %all-to-all-start.2 = ((f32[8,256,128]{2,1,0:T(8,128)}), f32[8,256,128]{2,1,0:T(8,128)S(1)}, u32[]{:S(2)}, u32[]{:S(2)}) async-start(f32[8,256,128]{2,1,0:T(8,128)} %get-tuple-element.36), calls=%async_computation.2 | async-start | bytes 2097152 | tf_op jit(solution)/shard_map/all_to_all | solution.py:570
  53.0 15.6 %shard_map.79.o_hbm = f32[32,256,128]{2,1,0:T(8,128)} custom-call(f32[256,32,128]{2,1,0:T(8,128)} %b_hbm.5, s32[256,256]{1,0:T(8,128)S(1)} %copy-done, f32[32,128]{1,0:T(8,128)S(1)} %copy-done.1, f32[256,128]{1,0:T(8,128)S(1)} %get-tuple-element.21.cols_ref, f32[10,256,128]{2,1,0:T(8,128)S(1)} %get-tuple-element.22.tab_ref, ...), custom_call_target="tpu_custom_call" | custom-call | flops 12000000000 | bytes 24000000 | tf_op jit(solution)/shard_map/pallas_call | solution.py:500
  68.6 0.0 all-to-all-done.2.rx_ref
  68.6 4.3 %shard_map.80 = f32[256,32,128]{2,1,0:T(8,128)} custom-call(f32[32,256,128]{2,1,0:T(8,128)} %shard_map.79.o_hbm, f32[8,256,128]{2,1,0:T(8,128)S(1)} %all-to-all-done.2.rx_ref, f32[256,128]{1,0:T(8,128)S(1)} %get-tuple-element.21.cols_ref, f32[10,256,128]{2,1,0:T(8,128)S(1)} %get-tuple-element.22.tab_ref), custom_call_target="tpu_custom_call" | custom-call | flops 3000000000 | bytes 6000000 | tf_op jit(solution)/shard_map/pallas_call | solution.py:500
Async XLA Ops:
  0.0 11.2 %copy-start = (s32[256,256]{1,0:T(8,128)S(1)}, s32[256,256]{1,0:T(8,128)}, u32[]{:S(2)}) copy-start(s32[256,256]{1,0:T(8,128)} %adj_ref.3) | copy-start | bytes 786436
  0.0 11.2 %copy-start.1 = (f32[32,128]{1,0:T(8,128)S(1)}, f32[32,128]{1,0:T(8,128)}, u32[]{:S(2)}) copy-start(f32[32,128]{1,0:T(8,128)} %cap_ref.3) | copy-start | bytes 49156
  5.0 19.5 %all-to-all-start = ((f32[8,256,128]{2,1,0:T(8,128)}), f32[8,256,128]{2,1,0:T(8,128)S(1)}, u32[]{:S(2)}, u32[]{:S(2)}) async-start(f32[8,256,128]{2,1,0:T(8,128)} %get-tuple-element.24), calls=%async_computation | async-start | bytes 2097152 | tf_op jit(solution)/shard_map/all_to_all | solution.py:541
  26.1 16.2 %all-to-all-start.1 = ((f32[8,128,128]{2,1,0:T(8,128)}), f32[8,128,128]{2,1,0:T(8,128)S(1)}, u32[]{:S(2)}, u32[]{:S(2)}) async-start(f32[8,128,128]{2,1,0:T(8,128)} %get-tuple-element.29), calls=%async_computation.1 | async-start | bytes 1048576 | tf_op jit(solution)/shard_map/all_to_all | solution.py:557
  42.7 4.4 %collective-permute-start = (f32[2,128,128]{2,1,0:T(8,128)S(1)}, f32[2,128,128]{2,1,0:T(8,128)S(1)}, u32[]{:S(2)}, u32[]{:S(2)}) collective-permute-start(f32[2,128,128]{2,1,0:T(8,128)S(1)} %get-tuple-element.33), channel_id=1, source_target_pairs={{0,1},{1,0},{2,3},{3,2},{4,5},{5,4},{6,7},{7,6},{8,9},{9,8},{10,11... | collective-permute-start | bytes 393224 | tf_op jit(solution)/shard_map/ppermute | solution.py:566
  48.6 20.0 %all-to-all-start.2 = ((f32[8,256,128]{2,1,0:T(8,128)}), f32[8,256,128]{2,1,0:T(8,128)S(1)}, u32[]{:S(2)}, u32[]{:S(2)}) async-start(f32[8,256,128]{2,1,0:T(8,128)} %get-tuple-element.36), calls=%async_computation.2 | async-start | bytes 2097152 | tf_op jit(solution)/shard_map/all_to_all | solution.py:570

commit v5 on v4

--- a/solution.py
+++ b/solution.py
@@ -374,17 +374,27 @@
     coef = jnp.concatenate([top, bottom], axis=0)
     coef = coef + tab_ref[TURN] * pltpu.roll(own_ref[...] + tab_ref[HOP_Y] * coef, 96, 1)
     coef_ref[...] = coef
-    lane = lanes(S)
-    at_front, at_back = coef * tab_ref[DOWN], coef * tab_ref[UP]
-    front, back = tail_ref[0], tail_ref[1]
-    for k, table in enumerate(GROUPS):
-        inside = (lane >= 32 * k) & (lane < 32 * (k + 1))
-        weight = tab_ref[table]
-        front = front + lane_sum(jnp.where(inside, at_front, 0.0)) * weight
-        back = back + lane_sum(jnp.where(inside, at_back, 0.0)) * weight
-    sides[1] = front
-    sides[0] = back
-    send_messages(sides, msg_hbm, msems, mx, 8, column_slot)
+    lane = lanes(S // 2)
+    copies = []
+    for h in range(2):
+        part = pl.ds(h * (S // 2), S // 2)
+        at_front, at_back = coef_ref[part, :] * tab_ref[DOWN, part, :], coef_ref[part, :] * tab_ref[UP, part, :]
+        front, back = tail_ref[0, part, :], tail_ref[1, part, :]
+        for k, table in enumerate(GROUPS):
+            inside = (lane >= 32 * k) & (lane < 32 * (k + 1))
+            weight = tab_ref[table, part, :]
+            front = front + lane_sum(jnp.where(inside, at_front, 0.0)) * weight
+            back = back + lane_sum(jnp.where(inside, at_back, 0.0)) * weight
+        sides[1, part, :] = front
+        sides[0, part, :] = back
+        for k in range(8):
+            side = (k > mx).astype(jnp.int32)
+            target = msg_hbm.at[column_slot(k), part, :]
+            copy = pltpu.make_async_copy(sides.at[side, part, :], target, msems.at[h, k])
+            copy.start()
+            copies.append(copy)
+    for copy in copies:
+        copy.wait()
 
 
 def second_kernel(
@@ -412,11 +422,11 @@
             column_in(b_hbm, out_ref, b_sems, x).wait()
             plane_in(mid_hbm, mid_ref, m_sems, x).wait()
             plane_in(p_hbm, v_ref, p_sems, x).wait()
+        coef = roll_ref[...]
+        roll_ref[...] = pltpu.roll(coef, NYL - BR, 1)
         for j in range(BR):
             x = i * BR + j
-            coef = roll_ref[...]
-            cfu, cfm, cbu, cbm = (coef[:, 32 * k : 32 * k + 1] for k in range(4))
-            roll_ref[...] = pltpu.roll(coef, 127, 1)
+            cfu, cfm, cbu, cbm = (coef[:, 32 * k + j : 32 * k + j + 1] for k in range(4))
             mid = mid_ref[x] + c * (cfu * ef + cbu * eb)
             v = v_ref[x] + cfu * alpha + cbu * beta + cfm * ef + cbm * eb
             v_ref[x] = v
@@ -565,7 +575,7 @@
     part, msg = call(chips_kernel, [(ry, VM), (in_vmem(sides), VM), tab, (in_vmem(tail), VM)], [halves_out, to_core], [], 1)
     other = lax.ppermute(msg, "gy", other_core)
     coef, msg = call(
-        columns_kernel, [(in_vmem(part), VM), (other, VM), (in_vmem(own), VM), (in_vmem(tail), VM), tab], [plane_out, x_out], x_sides, 1
+        columns_kernel, [(in_vmem(part), VM), (other, VM), (in_vmem(own), VM), (in_vmem(tail), VM), tab], [plane_out, x_out], [x_sides[0], pltpu.SemaphoreType.DMA((2, 8))], 1
     )
     rx = in_vmem(lax.all_to_all(msg, ("gx", "gy"), 0, 0, axis_index_groups=same_row))
     (part,) = call(

time: 73.2 us -> 71.8 us (0.981)
  Pallas kernels: 48.4 us -> 47.1 us
    pallas_call x8, Pallas kernels: 48.4 us -> 47.1 us  [call(): pl.pallas_call(kernel, out_shape=[shape for shape, _ in outs], in_specs=[...]
  transfers between devices with their start and end apart: 4 -> 4, of which waited for: 3 -> 3; matrix products, arithmetic and copies ran while one was open for 0% -> 0% of each run, Pallas kernels for 49% -> 48%
where the time goes in v5:
time: 71.8 us; the launch traced here: 71.5 us
  Pallas kernels  47.1 us (66%)
  starting transfers between devices  21.4 us (30%)
  waiting for transfers between devices  2.98 us (4%)
    pallas_call x8, Pallas kernels, call(): pl.pallas_call(kernel, out_shape=[shape for shape, _ in outs], in_specs=[...  47.1 us
    all_to_all x2, starting transfers between devices, shards(): lax.all_to_all(msg, ('gx', 'gy'), 0, 0, axis_index_groups=same_row)  10.5 us
    all_to_all x1, starting transfers between devices, shards(): ry = in_vmem(lax.all_to_all(msg, 'gy', 0, 0, axis_index_groups=same_core))  7.38 us
    ppermute x1, starting transfers between devices, shards(): other = lax.ppermute(msg, 'gy', other_core)  3.45 us
    all_to_all x1, waiting for transfers between devices, shards(): ry = in_vmem(lax.all_to_all(msg, 'gy', 0, 0, axis_index_groups=same_core))  1.55 us
  transfers between devices with their start and end apart: 4, of which 3 were waited for; matrix products, arithmetic and copies ran while one was open for 0% of the time, Pallas kernels for 48%

profile of v5, /device:TPU:1, one launch (start us, length us, event | category | flops | bytes accessed | tf_op | source)
XLA Modules:
  0.0 71.5 jit_solution(4613243115241446712)
XLA Ops:
  0.0 0.0 copy-start
  0.0 0.0 copy-start.1
  0.0 5.0 %shard_map.73 = (f32[256,128]{1,0:T(8,128)S(1)}, f32[8,256,128]{2,1,0:T(8,128)}) custom-call(f32[256,32,128]{2,1,0:T(8,128)} %b_hbm.5, s32[1,256]{1,0:T(1,128)} %bitcast.4, f32[1,256]{1,0:T(1,128)} %bitcast.5, f32[1,256]{1,0:T(1,128)} %bitcast.6, f32[1,256]{1,0:T(1,128)} %bitcast.7), custom_call_target="tpu_custom_call" | custom-call | flops 3000000000 | bytes 6000000 | tf_op jit(solution)/shard_map/pallas_call | solution.py:510
  5.0 6.2 %all-to-all-start = ((f32[8,256,128]{2,1,0:T(8,128)}), f32[8,256,128]{2,1,0:T(8,128)S(1)}, u32[]{:S(2)}, u32[]{:S(2)}) async-start(f32[8,256,128]{2,1,0:T(8,128)} %get-tuple-element.24), calls=%async_computation | async-start | bytes 2097152 | tf_op jit(solution)/shard_map/all_to_all | solution.py:551
  11.2 0.0 copy-done
  11.2 0.0 copy-done.1
  11.2 12.9 %shard_map.74 = (f32[32,256,128]{2,1,0:T(8,128)}, f32[256,128]{1,0:T(8,128)S(1)}, f32[10,256,128]{2,1,0:T(8,128)S(1)}) custom-call(f32[256,32,128]{2,1,0:T(8,128)} %b_hbm.5, s32[256,256]{1,0:T(8,128)S(1)} %copy-done, f32[32,128]{1,0:T(8,128)S(1)} %copy-done.1, f32[256,128]{1,0:T(8,128)S(1)} %get-tuple-element.21.cols_ref), custom_call_target="tpu_custom_call" | custom-call | flops 12000000000 | bytes 24000000 | tf_op jit(solution)/shard_map/pallas_call | solution.py:510
  24.1 0.4 all-to-all-done.rx_ref
  24.5 1.6 %shard_map.75 = (f32[2,256,128]{2,1,0:T(8,128)S(1)}, f32[256,128]{1,0:T(8,128)S(1)}, f32[2,128,128]{2,1,0:T(8,128)S(1)}, f32[8,128,128]{2,1,0:T(8,128)}) custom-call(f32[8,256,128]{2,1,0:T(8,128)S(1)} %all-to-all-done.rx_ref, f32[256,128]{1,0:T(8,128)S(1)} %get-tuple-element.25.fun_ref, f32[10,256,128]{2,1,0:T(8,128)S(1)} %get-tuple-element.22.tab_ref), custom_call_target="tpu_custom_call" | custom-call | flops 1000000000 | bytes 2000000 | tf_op jit(solution)/shard_map/pallas_call | solution.py:510
  26.1 7.4 %all-to-all-start.1 = ((f32[8,128,128]{2,1,0:T(8,128)}), f32[8,128,128]{2,1,0:T(8,128)S(1)}, u32[]{:S(2)}, u32[]{:S(2)}) async-start(f32[8,128,128]{2,1,0:T(8,128)} %get-tuple-element.29), calls=%async_computation.1 | async-start | bytes 1048576 | tf_op jit(solution)/shard_map/all_to_all | solution.py:567
  33.5 7.3 %shard_map.76 = (f32[32,256,128]{2,1,0:T(8,128)}, f32[32,256,128]{2,1,0:T(8,128)}, f32[2,256,128]{2,1,0:T(8,128)S(1)}) custom-call(f32[32,256,128]{2,1,0:T(8,128)} %get-tuple-element.23.q_hbm, f32[2,256,128]{2,1,0:T(8,128)S(1)} %get-tuple-element.26.car_ref, f32[256,128]{1,0:T(8,128)S(1)} %get-tuple-element.21.cols_ref), custom_call_target="tpu_custom_call" | custom-call | flops 12000000000 | bytes 24000000 | tf_op jit(solution)/shard_map/pallas_call | solution.py:510
  40.8 1.6 %all-to-all-done.1.ry_ref = f32[8,128,128]{2,1,0:T(8,128)S(1)} async-done(((f32[8,128,128]{2,1,0:T(8,128)}), f32[8,128,128]{2,1,0:T(8,128)S(1)}, u32[]{:S(2)}, u32[]{:S(2)}) %all-to-all-start.1) | async-done | bytes 524320 | tf_op jit(solution)/shard_map/all_to_all | solution.py:567
  42.3 0.3 shard_map.77
  42.7 3.4 %collective-permute-start = (f32[2,128,128]{2,1,0:T(8,128)S(1)}, f32[2,128,128]{2,1,0:T(8,128)S(1)}, u32[]{:S(2)}, u32[]{:S(2)}) collective-permute-start(f32[2,128,128]{2,1,0:T(8,128)S(1)} %get-tuple-element.33), channel_id=1, source_target_pairs={{0,1},{1,0},{2,3},{3,2},{4,5},{5,4},{6,7},{7,6},{8,9},{9,8},{10,11... | collective-permute-start | bytes 393224 | tf_op jit(solution)/shard_map/ppermute | solution.py:576
  46.1 1.0 %collective-permute-done.other_ref = f32[2,128,128]{2,1,0:T(8,128)S(1)} collective-permute-done((f32[2,128,128]{2,1,0:T(8,128)S(1)}, f32[2,128,128]{2,1,0:T(8,128)S(1)}, u32[]{:S(2)}, u32[]{:S(2)}) %collective-permute-start) | collective-permute-done | bytes 131104 | tf_op jit(solution)/shard_map/ppermute | solution.py:576
  47.1 1.4 %shard_map.78 = (f32[256,128]{1,0:T(8,128)S(1)}, f32[8,256,128]{2,1,0:T(8,128)}) custom-call(f32[2,128,128]{2,1,0:T(8,128)S(1)} %get-tuple-element.32.part_ref, f32[2,128,128]{2,1,0:T(8,128)S(1)} %collective-permute-done.other_ref, f32[256,128]{1,0:T(8,128)S(1)} %get-tuple-element.34.own_ref, f32[2,256,128]{2,1,0:T(8,128)S(1)} %get-tuple-element.31.tail_ref, ...), custom_call_target="tpu_custom_call" | custom-call | flops 1000000000 | bytes 2000000 | tf_op jit(solution)/shard_map/pallas_call | solution.py:510
  48.5 4.3 %all-to-all-start.2 = ((f32[8,256,128]{2,1,0:T(8,128)}), f32[8,256,128]{2,1,0:T(8,128)S(1)}, u32[]{:S(2)}, u32[]{:S(2)}) async-start(f32[8,256,128]{2,1,0:T(8,128)} %get-tuple-element.36), calls=%async_computation.2 | async-start | bytes 2097152 | tf_op jit(solution)/shard_map/all_to_all | solution.py:580
  52.9 14.3 %shard_map.79.o_hbm = f32[32,256,128]{2,1,0:T(8,128)} custom-call(f32[256,32,128]{2,1,0:T(8,128)} %b_hbm.5, s32[256,256]{1,0:T(8,128)S(1)} %copy-done, f32[32,128]{1,0:T(8,128)S(1)} %copy-done.1, f32[256,128]{1,0:T(8,128)S(1)} %get-tuple-element.21.cols_ref, f32[10,256,128]{2,1,0:T(8,128)S(1)} %get-tuple-element.22.tab_ref, ...), custom_call_target="tpu_custom_call" | custom-call | flops 12000000000 | bytes 24000000 | tf_op jit(solution)/shard_map/pallas_call | solution.py:510
  67.2 0.0 all-to-all-done.2.rx_ref
  67.2 4.3 %shard_map.80 = f32[256,32,128]{2,1,0:T(8,128)} custom-call(f32[32,256,128]{2,1,0:T(8,128)} %shard_map.79.o_hbm, f32[8,256,128]{2,1,0:T(8,128)S(1)} %all-to-all-done.2.rx_ref, f32[256,128]{1,0:T(8,128)S(1)} %get-tuple-element.21.cols_ref, f32[10,256,128]{2,1,0:T(8,128)S(1)} %get-tuple-element.22.tab_ref), custom_call_target="tpu_custom_call" | custom-call | flops 3000000000 | bytes 6000000 | tf_op jit(solution)/shard_map/pallas_call | solution.py:510
Async XLA Ops:
  0.0 11.2 %copy-start = (s32[256,256]{1,0:T(8,128)S(1)}, s32[256,256]{1,0:T(8,128)}, u32[]{:S(2)}) copy-start(s32[256,256]{1,0:T(8,128)} %adj_ref.3) | copy-start | bytes 786436
  0.0 11.2 %copy-start.1 = (f32[32,128]{1,0:T(8,128)S(1)}, f32[32,128]{1,0:T(8,128)}, u32[]{:S(2)}) copy-start(f32[32,128]{1,0:T(8,128)} %cap_ref.3) | copy-start | bytes 49156
  5.0 19.5 %all-to-all-start = ((f32[8,256,128]{2,1,0:T(8,128)}), f32[8,256,128]{2,1,0:T(8,128)S(1)}, u32[]{:S(2)}, u32[]{:S(2)}) async-start(f32[8,256,128]{2,1,0:T(8,128)} %get-tuple-element.24), calls=%async_computation | async-start | bytes 2097152 | tf_op jit(solution)/shard_map/all_to_all | solution.py:551
  26.1 16.2 %all-to-all-start.1 = ((f32[8,128,128]{2,1,0:T(8,128)}), f32[8,128,128]{2,1,0:T(8,128)S(1)}, u32[]{:S(2)}, u32[]{:S(2)}) async-start(f32[8,128,128]{2,1,0:T(8,128)} %get-tuple-element.29), calls=%async_computation.1 | async-start | bytes 1048576 | tf_op jit(solution)/shard_map/all_to_all | solution.py:567
  42.7 4.4 %collective-permute-start = (f32[2,128,128]{2,1,0:T(8,128)S(1)}, f32[2,128,128]{2,1,0:T(8,128)S(1)}, u32[]{:S(2)}, u32[]{:S(2)}) collective-permute-start(f32[2,128,128]{2,1,0:T(8,128)S(1)} %get-tuple-element.33), channel_id=1, source_target_pairs={{0,1},{1,0},{2,3},{3,2},{4,5},{5,4},{6,7},{7,6},{8,9},{9,8},{10,11... | collective-permute-start | bytes 393224 | tf_op jit(solution)/shard_map/ppermute | solution.py:576
  48.5 18.7 %all-to-all-start.2 = ((f32[8,256,128]{2,1,0:T(8,128)}), f32[8,256,128]{2,1,0:T(8,128)S(1)}, u32[]{:S(2)}, u32[]{:S(2)}) async-start(f32[8,256,128]{2,1,0:T(8,128)} %get-tuple-element.36), calls=%async_computation.2 | async-start | bytes 2097152 | tf_op jit(solution)/shard_map/all_to_all | solution.py:580
